TPU v7x, 32 devices: a whole 2x2x4 slice. The times are simulated.
32 devices in a mesh: wa: 8 (over z, x), gx: 4 (over y, core).
Axes of the slice: x: 2, y: 2, z: 4, core: 2. Of those that a mesh axis runs over, the one named last changes fastest.
Arguments:
- field_a: float32 [2, 4, 768, 3840], P(None, 'gx', 'wa'), may hold values from -6 to 6
- field_b: float32 [2, 4, 768, 3840], P(None, 'gx', 'wa'), may hold values from -6 to 6
- keep_mask: int32 [3840], replicated, may hold values 0 or 1
- block_inv: float32 [6, 128, 128], replicated
- lower_mult: float32 [5, 128, 128], replicated, may hold values from -0.15 to 0.15
Outputs:
- new_a: float32 [2, 4, 768, 3840], P(None, 'gx', 'wa')
- new_b: float32 [2, 4, 768, 3840], P(None, 'gx', 'wa')
All inputs are finite; a program needn't handle non-finite values.
Results may differ from a plain program's by a relative error of at most 0.0001.
Values sent between devices are 32-bit elements; how exact they have to be, the bound alone decides.
A program may use at most 192 MiB of HBM per device.

v0:
```python
import math

import jax
import jax.numpy as jnp
from jax import lax
from jax.sharding import PartitionSpec as P

NL_COEFF = 0.25


def product_high(form, left, right):
    return jnp.einsum(form, left, right, precision=lax.Precision.HIGHEST)


def dft_tables(length, direction):
    outer = math.gcd(length, 128)
    inner = length // outer
    outer_idx = jnp.arange(outer, dtype=jnp.int32)
    inner_idx = jnp.arange(inner, dtype=jnp.int32)
    angle_outer = (
        2.0
        * math.pi
        / outer
        * (outer_idx[:, None] * outer_idx[None, :] % outer).astype(jnp.float32)
    )
    angle_inner = (
        2.0
        * math.pi
        / inner
        * (inner_idx[:, None] * inner_idx[None, :] % inner).astype(jnp.float32)
    )
    angle_twist = (
        2.0
        * math.pi
        / length
        * (outer_idx[:, None] * inner_idx[None, :] % length).astype(jnp.float32)
    )
    return (
        outer,
        inner,
        jnp.cos(angle_outer),
        direction * jnp.sin(angle_outer),
        jnp.cos(angle_twist),
        direction * jnp.sin(angle_twist),
        jnp.cos(angle_inner),
        direction * jnp.sin(angle_inner),
    )


def transform(real_part, imag_part, tables):
    outer, inner, cos_outer, sin_outer, cos_twist, sin_twist, cos_inner, sin_inner = tables
    leading = real_part.shape[:-1]
    length = real_part.shape[-1]
    split_re = real_part.reshape(leading + (outer, inner))
    split_im = imag_part.reshape(leading + (outer, inner))
    section_re = product_high("...ab,ac->...cb", split_re, cos_outer) - product_high(
        "...ab,ac->...cb", split_im, sin_outer
    )
    section_im = product_high("...ab,ac->...cb", split_re, sin_outer) + product_high(
        "...ab,ac->...cb", split_im, cos_outer
    )
    twist_re = section_re * cos_twist - section_im * sin_twist
    twist_im = section_re * sin_twist + section_im * cos_twist
    final_re = product_high("...cb,bd->...cd", twist_re, cos_inner) - product_high(
        "...cb,bd->...cd", twist_im, sin_inner
    )
    final_im = product_high("...cb,bd->...cd", twist_re, sin_inner) + product_high(
        "...cb,bd->...cd", twist_im, cos_inner
    )
    final_re = jnp.swapaxes(final_re, -1, -2).reshape(leading + (length,))
    final_im = jnp.swapaxes(final_im, -1, -2).reshape(leading + (length,))
    return (final_re, final_im)


def to_grid(field, tables):
    modes = field.shape[-1]
    half = modes // 2
    length = 3 * modes // 2
    padding = jnp.zeros(field.shape[1:-1] + (length - modes,), jnp.float32)
    padded_re = jnp.concatenate([field[0, ..., :half], padding, field[0, ..., half:]], axis=-1)
    padded_im = jnp.concatenate([field[1, ..., :half], padding, field[1, ..., half:]], axis=-1)
    grid_re, grid_im = transform(padded_re, padded_im, tables)
    scale = 1.0 / math.sqrt(modes)
    return jnp.stack([grid_re * scale, grid_im * scale])


def to_modes(values, tables, modes):
    length = values.shape[-1]
    half = modes // 2
    spec_re, spec_im = transform(values[0], values[1], tables)
    scale = 1.0 / math.sqrt(length)
    kept_re = jnp.concatenate([spec_re[..., :half], spec_re[..., length - half :]], axis=-1) * scale
    kept_im = jnp.concatenate([spec_im[..., :half], spec_im[..., length - half :]], axis=-1) * scale
    return jnp.stack([kept_re, kept_im])


def complex_product(left, right):
    return jnp.stack(
        [left[0] * right[0] - left[1] * right[1], left[0] * right[1] + left[1] * right[0]]
    )


def convolve(grid_a, grid_b, first_mode, count):
    total = grid_a.shape[1]
    mine = first_mode + jnp.arange(count, dtype=jnp.int32)
    zeros_like_mine = jnp.zeros((2, count) + grid_a.shape[2:], jnp.float32)

    def step(offset, sums):
        sum_p, sum_q = sums
        own_a = lax.dynamic_slice_in_dim(grid_a, offset, 1, 1)
        own_b = lax.dynamic_slice_in_dim(grid_b, offset, 1, 1)
        partner = jnp.mod(mine - offset, total)
        other_a = jnp.take(grid_a, partner, axis=1)
        other_b = jnp.take(grid_b, partner, axis=1)
        sum_p = sum_p + complex_product(own_a, other_b)
        sum_q = sum_q + complex_product(own_a, other_a) - complex_product(own_b, other_b)
        return (sum_p, sum_q)

    return lax.fori_loop(0, total, step, (zeros_like_mine, zeros_like_mine))


def solve_rows(rhs, block_inv, lower_mult):
    shape = rhs.shape
    nblocks = block_inv.shape[0]
    width = block_inv.shape[1]
    vectors = jnp.swapaxes(rhs, 2, 3).reshape(-1, nblocks, width)
    blocks = jnp.moveaxis(vectors, 1, 0)

    def forward(previous, inputs):
        current, multiplier = inputs
        result = current - product_high("mc,rc->mr", previous, multiplier)
        return (result, result)

    _, later = lax.scan(forward, blocks[0], (blocks[1:], lower_mult))
    reduced = jnp.concatenate([blocks[:1], later], axis=0)
    last = product_high("mc,rc->mr", reduced[-1], block_inv[-1])

    def backward(following, inputs):
        current, inverse, multiplier = inputs
        result = product_high("mc,rc->mr", current, inverse) - product_high(
            "mc,cr->mr", following, multiplier
        )
        return (result, result)

    _, earlier = lax.scan(backward, last, (reduced[:-1], block_inv[:-1], lower_mult), reverse=True)
    solved = jnp.concatenate([earlier, last[None]], axis=0)
    solved = jnp.moveaxis(solved, 0, 1).reshape(shape[0], shape[1], shape[3], shape[2])
    return jnp.swapaxes(solved, 2, 3)


def body(field_a, field_b, keep_mask, block_inv, lower_mult):
    modes = field_a.shape[3]
    length = 3 * modes // 2
    inverse_tables = dft_tables(length, 1.0)
    forward_tables = dft_tables(length, -1.0)
    keep = keep_mask.astype(jnp.float32)
    local_count = field_a.shape[1]
    first_mode = lax.axis_index("gx") * local_count
    own_grid_a = to_grid(field_a, inverse_tables)
    own_grid_b = to_grid(field_b, inverse_tables)
    grid_a, grid_b = (
        lax.all_gather(own_grid_a, "gx", axis=1, tiled=True),
        lax.all_gather(own_grid_b, "gx", axis=1, tiled=True),
    )
    prod_p, prod_q = convolve(grid_a, grid_b, first_mode, local_count)
    rhs_a = field_a + NL_COEFF * to_modes(prod_p, forward_tables, modes) * keep
    rhs_b = field_b + NL_COEFF * to_modes(prod_q, forward_tables, modes) * keep
    solved_a = solve_rows(
        lax.all_to_all(rhs_a, "wa", split_axis=3, concat_axis=2, tiled=True), block_inv, lower_mult
    )
    solved_b = solve_rows(
        lax.all_to_all(rhs_b, "wa", split_axis=3, concat_axis=2, tiled=True), block_inv, lower_mult
    )
    new_a, new_b = (
        lax.all_to_all(solved_a, "wa", split_axis=2, concat_axis=3, tiled=True),
        lax.all_to_all(solved_b, "wa", split_axis=2, concat_axis=3, tiled=True),
    )
    return (new_a, new_b)


def solution(mesh):
    return jax.shard_map(
        body,
        mesh=mesh,
        in_specs=(P(None, "gx", "wa", None), P(None, "gx", "wa", None), P(), P(), P()),
        out_specs=(P(None, "gx", "wa", None), P(None, "gx", "wa", None)),
        check_vma=False,
    )
```

profile of v0, /device:TPU:4, one launch (start us, length us, event | category | flops | bytes accessed | tf_op | source)
XLA Modules:
  0.0 992.4 jit_solution(6693306750218715234)
XLA Ops:
  13.6 8.9 reshape.732
  22.6 4.9 copy.146
  34.5 10.0 %reshape.730 = f32[96,128,45]{2,1,0:T(8,128)} reshape(f32[1,96,5760]{2,1,0:T(8,128)} %get-tuple-element.644) | data formatting | bytes 4423680 | tf_op jit(solution)/shard_map/reshape.2
  44.5 5.3 copy.136
  57.1 10.0 %reshape.731 = f32[96,128,45]{2,1,0:T(8,128)} reshape(f32[1,96,5760]{2,1,0:T(8,128)} %get-tuple-element.642) | data formatting | bytes 4423680 | tf_op jit(solution)/shard_map/reshape.4
  67.1 6.2 copy.138
  73.3 8.9 reshape.733
  82.3 5.0 copy.148
  104.3 5.1 fusion.47
  109.4 5.4 multiply_bitcast_fusion.1
  117.6 7.6 multiply_bitcast_fusion
  133.0 5.3 fusion.57
  138.4 5.5 multiply_bitcast_fusion.3
  147.3 5.9 fusion.55
  153.2 5.3 multiply_bitcast_fusion.2
  166.8 77.7 %all-gather.5.cloned.1.call-done = f32[2,4,96,5760]{3,2,1,0:T(8,128)} async-done(((f32[2,1,96,5760]{3,2,1,0:T(8,128)}), f32[2,4,96,5760]{3,2,1,0:T(8,128)}) %all-gather.5.cloned.1.call-update) | async-done | bytes 17694736 | tf_op jit(solution)/shard_map/all_gather | solution.py:163
  244.5 112.9 %all-gather.3.cloned.1.call-done = f32[2,4,96,5760]{3,2,1,0:T(8,128)} async-done(((f32[2,1,96,5760]{3,2,1,0:T(8,128)}), f32[2,4,96,5760]{3,2,1,0:T(8,128)}) %all-gather.3.cloned.1.call-update) | async-done | bytes 17694736 | tf_op jit(solution)/shard_map/all_gather | solution.py:162
  357.4 118.1 %while.79 = (s32[]{:T(128)}, f32[2,1,96,5760]{3,2,1,0:T(8,128)}, f32[2,1,96,5760]{3,2,1,0:T(8,128)}, f32[2,4,96,5760]{3,2,1,0:T(8,128)}, s32[1]{0:T(128)}, /*ind...) while((s32[]{:T(128)}, f32[2,1,96,5760]{3,2,1,0:T(8,128)}, ...), condition=%wide.region_1.3_spmd.clone, body=%wide.region_0.2_spmd.clone.sunk | while | flops 21012500 | bytes 88473952 | solution.py:119
  357.4 7.6 dynamic-slice_select_fusion.3
  365.0 10.7 %multiply_subtract_fusion.4 = (f32[1,1,96,5760]{3,2,1,0:T(8,128)}, f32[1,1,96,5760]{3,2,1,0:T(8,128)}, f32[1,1,96,5760]{3,2,1,0:T(8,128)S(1)}, f32[1,1,96,5760]{...) fusion(f32[2,1,96,5760]{3,2,1,0:T(8,128)} %get-tuple-element.850, ...), kind=kLoop, calls=%fused_computation.44.clone.1 | loop fusion | flops 9953280 | bytes 30965768 | tf_op jit(solution)/shard_map/while/body/eval_jaxpr/sub | solution.py:99
  375.7 5.4 fusion.437
  383.7 7.6 dynamic-slice_select_fusion.3
  391.3 10.7 %multiply_subtract_fusion.4 = (f32[1,1,96,5760]{3,2,1,0:T(8,128)}, f32[1,1,96,5760]{3,2,1,0:T(8,128)}, f32[1,1,96,5760]{3,2,1,0:T(8,128)S(1)}, f32[1,1,96,5760]{...) fusion(f32[2,1,96,5760]{3,2,1,0:T(8,128)} %get-tuple-element.850, ...), kind=kLoop, calls=%fused_computation.44.clone.1 | loop fusion | flops 9953280 | bytes 30965768 | tf_op jit(solution)/shard_map/while/body/eval_jaxpr/sub | solution.py:99
  402.1 7.4 fusion.437
  409.5 4.9 maximum_add_fusion.3
  414.3 7.6 dynamic-slice_select_fusion.3
  421.9 10.7 %multiply_subtract_fusion.4 = (f32[1,1,96,5760]{3,2,1,0:T(8,128)}, f32[1,1,96,5760]{3,2,1,0:T(8,128)}, f32[1,1,96,5760]{3,2,1,0:T(8,128)S(1)}, f32[1,1,96,5760]{...) fusion(f32[2,1,96,5760]{3,2,1,0:T(8,128)} %get-tuple-element.850, ...), kind=kLoop, calls=%fused_computation.44.clone.1 | loop fusion | flops 9953280 | bytes 30965768 | tf_op jit(solution)/shard_map/while/body/eval_jaxpr/sub | solution.py:99
  432.7 7.4 fusion.437
  440.1 4.9 maximum_add_fusion.3
  444.9 7.6 dynamic-slice_select_fusion.3
  452.5 10.7 %multiply_subtract_fusion.4 = (f32[1,1,96,5760]{3,2,1,0:T(8,128)}, f32[1,1,96,5760]{3,2,1,0:T(8,128)}, f32[1,1,96,5760]{3,2,1,0:T(8,128)S(1)}, f32[1,1,96,5760]{...) fusion(f32[2,1,96,5760]{3,2,1,0:T(8,128)} %get-tuple-element.850, ...), kind=kLoop, calls=%fused_computation.44.clone.1 | loop fusion | flops 9953280 | bytes 30965768 | tf_op jit(solution)/shard_map/while/body/eval_jaxpr/sub | solution.py:99
  463.2 7.4 fusion.437
  470.7 4.9 maximum_add_fusion.3
  479.5 8.9 reshape.736
  488.4 5.3 copy.176
  504.7 8.9 reshape.734
  513.7 4.9 copy.156
  525.6 10.0 %reshape.735 = f32[96,128,45]{2,1,0:T(8,128)} reshape(f32[1,1,96,5760]{3,2,1,0:T(8,128)} %get-tuple-element.615) | data formatting | bytes 4423680 | tf_op jit(solution)/shard_map/reshape.58
  535.6 6.3 copy.158
  541.9 8.9 reshape.737
  550.9 5.0 copy.178
  571.9 5.1 fusion.39
  576.9 5.1 fusion.33
  582.0 5.1 fusion.31
  587.1 5.4 subtract_bitcast_fusion.1
  597.8 6.8 add_bitcast_fusion.1
  610.1 5.2 subtract_bitcast_fusion
  620.8 5.2 add_bitcast_fusion
  635.6 8.9 copy.185
  644.5 5.7 all-to-all-start.2
  650.2 5.9 copy.165
  656.2 82.2 %all-to-all-done.2 = f32[2,1,96,3840]{2,1,0,3:T(1,128)} async-done(((f32[2,1,96,3840]{2,1,0,3:T(1,128)}), f32[2,1,96,3840]{2,1,0,3:T(1,128)}, u32[]{:S(2)}, u32[]{:S(2)}) %all-to-all-start.2) | async-done | bytes 2949152 | tf_op jit(solution)/shard_map/all_to_all | solution.py:172
  743.9 5.2 copy.186
  767.5 8.3 while.77
  779.8 11.1 %while.78 = (s32[]{:T(128)}, f32[960,128]{1,0:T(8,128)S(1)}, f32[5,960,128]{2,1,0:T(8,128)S(1)}, f32[5,960,128]{2,1,0:T(8,128)}, f32[5,128,128]{2,1,0:T(8,128)},...) while((s32[]{:T(128)}, f32[960,128]{1,0:T(8,128)S(1)}, f32[5,960,128]{2,1,0:T(8,128)S(1)}, ...), condition=%wide.region_9.11_spmd, body=%wide.region_8.10_spmd.sunk | while | flops 377610240 | bytes 4065377 | solution.py:145
  800.6 29.6 %all-to-all-done = f32[2,1,96,3840]{2,1,0,3:T(1,128)} async-done(((f32[2,1,96,3840]{2,1,0,3:T(1,128)}), f32[2,1,96,3840]{2,1,0,3:T(1,128)}, u32[]{:S(2)}, u32[]{:S(2)}) %all-to-all-start) | async-done | bytes 2949152 | tf_op jit(solution)/shard_map/all_to_all | solution.py:169
  830.2 4.9 all-to-all-start.3
  835.1 5.2 copy.166
  844.4 4.8 reshape.655
  858.6 8.3 while.75
  871.0 11.1 %while.76 = (s32[]{:T(128)}, f32[960,128]{1,0:T(8,128)S(1)}, f32[5,960,128]{2,1,0:T(8,128)S(1)}, f32[5,960,128]{2,1,0:T(8,128)}, f32[5,128,128]{2,1,0:T(8,128)},...) while((s32[]{:T(128)}, f32[960,128]{1,0:T(8,128)S(1)}, f32[5,960,128]{2,1,0:T(8,128)S(1)}, ...), condition=%wide.region_5.7_spmd, body=%wide.region_4.6_spmd.sunk | while | flops 377610240 | bytes 4065377 | solution.py:145
  891.8 13.5 %all-to-all-done.3 = f32[2,1,768,480]{3,0,1,2:T(2,128)} async-done(((f32[2,1,768,480]{3,0,1,2:T(2,128)}), f32[2,1,768,480]{3,0,1,2:T(2,128)}, u32[]{:S(2)}, u32[]{:S(2)}) %all-to-all-start.3) | async-done | bytes 2949152 | tf_op jit(solution)/shard_map/all_to_all | solution.py:176
  915.1 4.8 all_to_all.67
  919.9 60.0 %all-to-all-done.1 = f32[2,1,768,480]{3,0,1,2:T(2,128)S(1)} async-done(((f32[2,1,768,480]{3,0,1,2:T(2,128)}), f32[2,1,768,480]{3,0,1,2:T(2,128)S(1)}, u32[]{:S(2)}, u32[]{:S(2)}) %all-to-all-start.1) | async-done | bytes 2949152 | tf_op jit(solution)/shard_map/all_to_all | solution.py:175
  (214 shorter events, 244.5 us)
Async XLA Ops:
  7.2 237.3 %all-gather.5.cloned.1.call-start = ((), (), s32[]{:S(2)}) async-start(), calls=%async_computation.5 | async-start | bytes 22118400 | tf_op jit(solution)/shard_map/all_gather | solution.py:163
  57.1 38.8 %copy-start.30 = (f32[128,45]{0,1:T(8,128)}, f32[128,45]{0,1:T(8,128)S(1)}, u32[]{:S(2)}) copy-start(f32[128,45]{0,1:T(8,128)S(1)} %get-tuple-element.652) | copy-start | bytes 69124
  67.1 6.2 copy-start.14
  87.3 4.0 copy-start.11
  91.3 2.3 copy-start.4
  91.3 2.3 copy-start.12
  93.6 2.3 copy-start.17
  100.4 9.0 copy-start.3
  133.0 224.4 %all-gather.3.cloned.1.call-start = ((), (), s32[]{:S(2)}) async-start(), calls=%async_computation.4 | async-start | bytes 22118400 | tf_op jit(solution)/shard_map/all_gather | solution.py:162
  158.6 2.9 copy-start.16
  165.5 0.7 copy-start.33
  375.7 5.4 copy-start
  402.1 7.4 copy-start
  432.6 7.4 copy-start
  463.2 7.4 copy-start
  535.6 6.3 copy-start.15
  555.9 4.0 copy-start.10
  559.9 2.3 copy-start.5
  559.9 2.3 copy-start.13
  562.2 2.3 copy-start.18
  562.2 2.3 copy-start.31
  567.7 19.4 %copy-start.1 = (f32[96,128,45]{1,0,2:T(8,128)}, f32[96,128,45]{1,0,2:T(8,128)S(1)}, u32[]{:S(2)}) copy-start(f32[96,128,45]{1,0,2:T(8,128)S(1)} %get-tuple-element.638) | copy-start | bytes 6635524
  595.3 2.5 copy-start.2
  607.4 2.7 copy-start.9
  618.1 2.7 copy-start.8
  627.8 1.1 copy-start.22
  627.9 1.3 copy-start.23
  627.9 1.5 copy-start.24
  629.1 1.2 copy-start.25
  629.1 1.4 copy-start.26
  629.4 1.4 copy-start.32
  630.5 1.8 copy-start.7
  630.6 2.6 copy-start.6
  644.5 93.8 %all-to-all-start.2 = ((f32[2,1,96,3840]{2,1,0,3:T(1,128)}), f32[2,1,96,3840]{2,1,0,3:T(1,128)}, u32[]{:S(2)}, u32[]{:S(2)}) async-start(f32[2,1,96,3840]{2,1,0,3:T(1,128)} %copy.185), calls=%async_computation.2 | async-start | bytes 7864320 | tf_op jit(solution)/shard_map/all_to_all | solution.py:172
  656.1 87.0 %copy-start.29 = (f32[6,128,128]{2,1,0:T(8,128)S(1)}, f32[6,128,128]{2,1,0:T(8,128)}, u32[]{:S(2)}) copy-start(f32[6,128,128]{2,1,0:T(8,128)} %param.20) | copy-start | bytes 1179652
  738.3 91.9 %all-to-all-start = ((f32[2,1,96,3840]{2,1,0,3:T(1,128)}), f32[2,1,96,3840]{2,1,0,3:T(1,128)}, u32[]{:S(2)}, u32[]{:S(2)}) async-start(f32[2,1,96,3840]{2,1,0,3:T(1,128)} %copy.165), calls=%async_computation | async-start | bytes 7864320 | tf_op jit(solution)/shard_map/all_to_all | solution.py:169
  763.9 3.5 copy-start.19
  775.8 2.3 copy-start.27
  777.2 0.8 copy-start.21
  830.2 75.0 %all-to-all-start.3 = ((f32[2,1,768,480]{3,0,1,2:T(2,128)}), f32[2,1,768,480]{3,0,1,2:T(2,128)}, u32[]{:S(2)}, u32[]{:S(2)}) async-start(f32[2,1,768,480]{3,0,1,2:T(2,128)} %bitcast.110), calls=%async_computation.3 | async-start | bytes 6291456 | tf_op jit(solution)/shard_map/all_to_all | solution.py:176
  866.9 2.3 copy-start.28
  868.4 0.8 copy-start.20
  905.3 74.7 %all-to-all-start.1 = ((f32[2,1,768,480]{3,0,1,2:T(2,128)}), f32[2,1,768,480]{3,0,1,2:T(2,128)S(1)}, u32[]{:S(2)}, u32[]{:S(2)}) async-start(f32[2,1,768,480]{3,0,1,2:T(2,128)} %bitcast.82), calls=%async_computation.1 | async-start | bytes 6291456 | tf_op jit(solution)/shard_map/all_to_all | solution.py:175
Sparse Core Ops, SparseCore 0:
  133.1 111.3 all-gather.4
  246.1 111.3 all-gather.2
where the time goes:
time: 1000 us; the launch traced here: 992 us
  waiting for transfers between devices  376 us (38%)
  local copies, waits for them, and re-layouts  260 us (26%)
  matrix products  179 us (18%)
  other arithmetic  142 us (14%)
  starting transfers between devices  19.3 us (2%)
  between operations  14.9 us (1%)
    dot_general x64, matrix products, product_high(): return jnp.einsum(form, left, right, precision=lax.Precision.HIGHEST)  179 us
    another operation x21, local copies, waits for them, and re-layouts  118 us
    all_gather x1, waiting for transfers between devices, body(): lax.all_gather(own_grid_a, 'gx', axis=1, tiled=True)  113 us
    all_to_all x1, waiting for transfers between devices, body(): lax.all_to_all(rhs_b, 'wa', split_axis=3, concat_axis=2, tiled=True)  82.2 us
    all_gather x1, waiting for transfers between devices, body(): lax.all_gather(own_grid_b, 'gx', axis=1, tiled=True)  77.7 us
    all_to_all x1, waiting for transfers between devices, body(): lax.all_to_all(solved_a, 'wa', split_axis=2, concat_axis=3, tiled=True)  60 us
    sub x4, other arithmetic, complex_product(): left[0] * right[0] - left[1] * right[1]  43 us
    select_n x4, other arithmetic, step(): other_a = jnp.take(grid_a, partner, axis=1)  30.2 us
  transfers between devices with their start and end apart: 6, of which 6 were waited for; matrix products, arithmetic and copies ran while one was open for 16% of the time, Pallas kernels for 0%

commit v1 on v0

v1 whole, which is shorter than its diff:
```python
import functools
import math

import jax
import jax.numpy as jnp
import ml_dtypes
import numpy as np
from jax import lax
from jax.experimental import pallas as pl
from jax.experimental.pallas import tpu as pltpu
from jax.sharding import PartitionSpec as P

NL_COEFF = 0.25
LANES = 128
ROWS = 8
KXT = 4


def add(x, y):
    return (x[0] + y[0], x[1] + y[1])


def sub(x, y):
    return (x[0] - y[0], x[1] - y[1])


def scaled(x, factor):
    return (x[0] * factor, x[1] * factor)


def times_i(x, sign):
    return (-x[1], x[0]) if sign > 0 else (x[1], -x[0])


def times(x, re, im):
    return (x[0] * re - x[1] * im, x[0] * im + x[1] * re)


def dft3(x, sign):
    both, diff = add(x[1], x[2]), sub(x[1], x[2])
    mid = sub(x[0], scaled(both, 0.5))
    turn = times_i(scaled(diff, math.sqrt(0.75)), sign)
    return [add(x[0], both), add(mid, turn), sub(mid, turn)]


def dft4(x, sign):
    even, odd = add(x[0], x[2]), add(x[1], x[3])
    even_d, odd_d = sub(x[0], x[2]), times_i(sub(x[1], x[3]), sign)
    return [add(even, odd), add(even_d, odd_d), sub(even, odd), sub(even_d, odd_d)]


def dft5(x, sign):
    c1, c2 = math.cos(2 * math.pi / 5), math.cos(4 * math.pi / 5)
    s1, s2 = math.sin(2 * math.pi / 5), math.sin(4 * math.pi / 5)
    t1, t2 = add(x[1], x[4]), add(x[2], x[3])
    t3, t4 = sub(x[1], x[4]), sub(x[2], x[3])
    m1 = add(x[0], add(scaled(t1, c1), scaled(t2, c2)))
    m2 = add(x[0], add(scaled(t1, c2), scaled(t2, c1)))
    n1 = times_i(add(scaled(t3, s1), scaled(t4, s2)), sign)
    n2 = times_i(sub(scaled(t3, s2), scaled(t4, s1)), sign)
    return [add(x[0], add(t1, t2)), add(m1, n1), add(m2, n2), sub(m2, n2), sub(m1, n1)]


def dft9(x, sign):
    inner = [dft3([x[j], x[3 + j], x[6 + j]], sign) for j in range(3)]
    out = [None] * 9
    for d1 in range(3):
        terms = []
        for j in range(3):
            angle = sign * 2 * math.pi * j * d1 / 9
            term = inner[j][d1]
            terms.append(times(term, math.cos(angle), math.sin(angle)) if j * d1 else term)
        for d2, value in enumerate(dft3(terms, sign)):
            out[d1 + 3 * d2] = value
    return out


def dft45(load, store, mid_ref, sign, shape):
    zero = jnp.zeros(shape, jnp.float32)
    for beta in range(9):
        ins = [load((9 * alpha + 5 * beta) % 45) for alpha in range(5)]
        ins = [(zero, zero) if v is None else v for v in ins]
        for c, value in enumerate(dft5(ins, sign)):
            mid_ref[c, beta, 0], mid_ref[c, beta, 1] = value
    for c in range(5):
        outs = dft9([(mid_ref[c, b, 0], mid_ref[c, b, 1]) for b in range(9)], sign)
        for d in range(9):
            spot = next(b for b in range(45) if b % 5 == c and b % 9 == d)
            store(spot, outs[d])


def split_dot(x, w_hi, w_lo):
    hi = x.astype(jnp.bfloat16)
    lo = (x - hi.astype(jnp.float32)).astype(jnp.bfloat16)
    dot = functools.partial(jnp.dot, preferred_element_type=jnp.float32)
    return dot(hi, w_hi) + (dot(lo, w_hi) + dot(hi, w_lo))


def front_kernel(a_ref, b_ref, keep_ref, twist_ref, winv_ref, wfwd_ref, out_ref,
                 plane_ref, mid_ref, za_ref, zb_ref, hat_ref):
    half = 15
    tile = (ROWS, LANES)
    for f, ref in enumerate((a_ref, b_ref)):
        for t in range(30):
            cols = pl.ds(t * LANES, LANES)
            ins = [(ref[0, k, :, cols], ref[1, k, :, cols]) for k in range(KXT)]
            for x, value in enumerate(dft4(ins, 1)):
                plane_ref[x, f, t, 0], plane_ref[x, f, t, 1] = value

    def one_plane(x, carry):
        for f, z_ref in enumerate((za_ref, zb_ref)):
            def load(m1):
                if half <= m1 < 30:
                    return None
                t = m1 if m1 < half else m1 - half
                return (plane_ref[x, f, t, 0], plane_ref[x, f, t, 1])

            def store(b, value):
                re, im = times(value, twist_ref[0, b : b + 1, :], twist_ref[1, b : b + 1, :])
                z_ref[b * ROWS : (b + 1) * ROWS, :LANES] = re
                z_ref[b * ROWS : (b + 1) * ROWS, LANES:] = im

            dft45(load, store, mid_ref, 1, tile)
        grid_a = split_dot(za_ref[...], winv_ref[0], winv_ref[1])
        grid_b = split_dot(zb_ref[...], winv_ref[0], winv_ref[1])
        a = (grid_a[:, :LANES], grid_a[:, LANES:])
        b = (grid_b[:, :LANES], grid_b[:, LANES:])
        p = times(a, b[0], b[1])
        total, diff = add(a, b), sub(a, b)
        q = times(total, diff[0], diff[1])
        for z_ref, value in ((za_ref, p), (zb_ref, q)):
            z_ref[...] = split_dot(jnp.concatenate(value, axis=1), wfwd_ref[0], wfwd_ref[1])
        for f, z_ref in enumerate((za_ref, zb_ref)):
            def load(b):
                rows = slice(b * ROWS, (b + 1) * ROWS)
                value = (z_ref[rows, :LANES], z_ref[rows, LANES:])
                return times(value, twist_ref[0, b : b + 1, :], -twist_ref[1, b : b + 1, :])

            def store(m1, value):
                if half <= m1 < 30:
                    return
                t = m1 if m1 < half else m1 - half
                hat_ref[x, f, t, 0], hat_ref[x, f, t, 1] = value

            dft45(load, store, mid_ref, -1, tile)
        return carry

    lax.fori_loop(0, KXT, one_plane, 0)
    for f, ref in enumerate((a_ref, b_ref)):
        for t in range(30):
            cols = pl.ds(t * LANES, LANES)
            keep = keep_ref[:, cols]
            ins = [(hat_ref[x, f, t, 0], hat_ref[x, f, t, 1]) for x in range(KXT)]
            into = pl.ds(t % half * LANES, LANES)
            for k, value in enumerate(dft4(ins, -1)):
                for part in range(2):
                    out_ref[f, part, t // half, k, :, into] = (
                        ref[part, k, :, cols] + value[part] * keep
                    )


def front_tables(modes):
    length = 3 * modes // 2
    b, m2 = np.arange(length // LANES)[:, None], np.arange(LANES)[None, :]
    twist = 2 * np.pi * (b * m2 % length) / length
    lane = np.arange(LANES)
    w = 2 * np.pi * (lane[:, None] * lane[None, :] % LANES) / LANES
    c, s = np.cos(w), np.sin(w)
    inv = np.block([[c, s], [-s, c]]) / math.sqrt(modes)
    fwd = np.block([[c, -s], [s, c]]) * (NL_COEFF / KXT / math.sqrt(length))

    def halves(table):
        hi = table.astype(np.float32).astype(ml_dtypes.bfloat16)
        lo = (table - hi.astype(np.float64)).astype(np.float32).astype(ml_dtypes.bfloat16)
        return np.stack([hi, lo])

    return np.stack([np.cos(twist), np.sin(twist)]).astype(np.float32), halves(inv), halves(fwd)


def front(slab_a, slab_b, keep):
    _, kxt, rows, modes = slab_a.shape
    assert kxt == KXT and modes == 30 * LANES and rows % ROWS == 0
    twist, inv, fwd = front_tables(modes)
    points = 45
    field_spec = pl.BlockSpec((2, KXT, ROWS, modes), lambda i: (0, 0, i, 0))
    return pl.pallas_call(
        front_kernel,
        grid=(rows // ROWS,),
        out_shape=jax.ShapeDtypeStruct((2, 2, 2, KXT, rows, modes // 2), jnp.float32),
        in_specs=[
            field_spec,
            field_spec,
            pl.BlockSpec((1, modes), lambda i: (0, 0)),
            pl.BlockSpec(twist.shape, lambda i: (0, 0, 0)),
            pl.BlockSpec(inv.shape, lambda i: (0, 0, 0)),
            pl.BlockSpec(fwd.shape, lambda i: (0, 0, 0)),
        ],
        out_specs=pl.BlockSpec((2, 2, 2, KXT, ROWS, modes // 2), lambda i: (0, 0, 0, 0, i, 0)),
        scratch_shapes=[
            pltpu.VMEM((KXT, 2, 30, 2, ROWS, LANES), jnp.float32),
            pltpu.VMEM((5, 9, 2, ROWS, LANES), jnp.float32),
            pltpu.VMEM((points * ROWS, 2 * LANES), jnp.float32),
            pltpu.VMEM((points * ROWS, 2 * LANES), jnp.float32),
            pltpu.VMEM((KXT, 2, 30, 2, ROWS, LANES), jnp.float32),
        ],
        compiler_params=pltpu.CompilerParams(vmem_limit_bytes=40 * 1024 * 1024),
        cost_estimate=pl.CostEstimate(
            flops=rows * 32 * 5760 * 256 * 6, bytes_accessed=rows * 2**18, transcendentals=0
        ),
    )(slab_a, slab_b, keep, jnp.asarray(twist), jnp.asarray(inv), jnp.asarray(fwd))


def solve_matrix(block_inv, lower_mult):
    count, width = block_inv.shape[:2]
    dot = functools.partial(jnp.matmul, precision=lax.Precision.HIGHEST)
    eye = jnp.eye(count * width, dtype=jnp.float32).reshape(count, width, count * width)
    reduced = [eye[0]]
    for j in range(1, count):
        reduced.append(eye[j] - dot(lower_mult[j - 1], reduced[-1]))
    own = dot(block_inv, jnp.stack(reduced))
    solved = [own[-1]]
    for j in range(count - 2, -1, -1):
        solved.insert(0, own[j] - dot(lower_mult[j].T, solved[0]))
    return jnp.concatenate(solved, axis=0)


def body(wa, gx, field_a, field_b, keep_mask, block_inv, lower_mult):
    _, _, rows, modes = field_a.shape
    keep = keep_mask.astype(jnp.float32).reshape(1, modes)
    padded = -(-rows // (gx * ROWS)) * gx * ROWS
    share = padded // gx

    def spread(field):
        field = field.reshape(2, rows, modes)
        if padded != rows:
            field = jnp.pad(field, ((0, 0), (0, padded - rows), (0, 0)))
        field = field.reshape(2, gx, share, modes)
        return lax.all_to_all(field, "gx", split_axis=1, concat_axis=1, tiled=True)

    rhs = front(spread(field_a), spread(field_b), keep)
    chunks = wa // 4
    width = modes // chunks
    if chunks != 2:
        rhs = jnp.moveaxis(rhs, 2, 4).reshape(2, 2, KXT, share, chunks, width)
        rhs = jnp.moveaxis(rhs, 4, 2)
    rhs = rhs.reshape(wa * gx, share, width)
    rhs = lax.all_to_all(rhs, ("wa", "gx"), split_axis=0, concat_axis=0, tiled=True)
    rhs = rhs.reshape(wa, padded, width)[:, :rows].reshape(wa * rows, width)
    solved = jnp.matmul(
        solve_matrix(block_inv, lower_mult), rhs, precision=lax.Precision.HIGH
    ).reshape(wa, rows, width)
    solved = lax.all_to_all(solved, "wa", split_axis=0, concat_axis=0, tiled=True)
    solved = solved.reshape(2, 2, chunks, rows, width)
    solved = jnp.moveaxis(solved, 2, 3).reshape(2, 2, 1, rows, modes)
    return (solved[0], solved[1])


def solution(mesh):
    return jax.shard_map(
        functools.partial(body, mesh.shape["wa"], mesh.shape["gx"]),
        mesh=mesh,
        in_specs=(P(None, "gx", "wa", None), P(None, "gx", "wa", None), P(), P(), P()),
        out_specs=(P(None, "gx", "wa", None), P(None, "gx", "wa", None)),
        check_vma=False,
    )
```

time: 1000 us -> 408 us (0.41)
  local copies, waits for them, and re-layouts: 260 us -> 34.9 us
  waiting for transfers between devices: 376 us -> 182 us
  matrix products: 179 us -> 17.1 us
  other arithmetic: 142 us -> 0.33 us
  blocking collectives: 0 us -> 137 us
  Pallas kernels: 0 us -> 18.5 us
  between operations: 14.9 us -> 0.9 us
    all_gather x2 -> x0, waiting for transfers between devices: 191 us -> none  [the longest x1 113 us: body(): lax.all_gather(own_grid_a, 'gx', axis=1, tiled=True)]
    dot_general x64 -> x12, matrix products: 179 us -> 17.1 us  [the longest x1 9.98 us: body(): jnp.matmul(solve_matrix(block_inv, lower_mult), rhs, precision=lax.Precis...]
    all_to_all x0 -> x1, blocking collectives: none -> 137 us  [body(): lax.all_to_all(solved, 'wa', split_axis=0, concat_axis=0, tiled=True)]
    another operation x21 -> x2, local copies, waits for them, and re-layouts: 118 us -> 7.39 us  [spread(): field = field.reshape(2, gx, share, modes)]
    sub x8 -> x0, other arithmetic: 70.6 us -> none  [the longest x4 43 us: complex_product(): left[0] * right[0] - left[1] * right[1]]
    select_n x4 -> x0, other arithmetic: 30.2 us -> none  [step(): other_a = jnp.take(grid_a, partner, axis=1)]
    reshape x8 -> x1, local copies, waits for them, and re-layouts: 28.9 us -> 0.01 us  [body(): keep = keep_mask.astype(jnp.float32).reshape(1, modes)]
    all_to_all x8 -> x2, local copies, waits for them, and re-layouts: 26.7 us -> 4.13 us  [spread(): return lax.all_to_all(field, 'gx', split_axis=1, concat_axis=1, tiled=True)]
  transfers between devices with their start and end apart: 6 -> 3, of which waited for: 6 -> 3; matrix products, arithmetic and copies ran while one was open for 16% -> 3% of each run, Pallas kernels for 0% -> 0%
where the time goes in v1:
time: 408 us; the launch traced here: 407 us
  waiting for transfers between devices  182 us (45%)
  blocking collectives  137 us (34%)
  local copies, waits for them, and re-layouts  34.9 us (9%)
  Pallas kernels  18.5 us (5%)
  starting transfers between devices  17.1 us (4%)
  matrix products  17.1 us (4%)
    all_to_all x1, blocking collectives, body(): lax.all_to_all(solved, 'wa', split_axis=0, concat_axis=0, tiled=True)  137 us
    all_to_all x1, waiting for transfers between devices, body(): lax.all_to_all(rhs, ('wa', 'gx'), split_axis=0, concat_axis=0, tiled=True)  122 us
    all_to_all x2, waiting for transfers between devices, spread(): return lax.all_to_all(field, 'gx', split_axis=1, concat_axis=1, tiled=True)  60.3 us
    pallas_call x1, Pallas kernels, front(): pl.pallas_call(front_kernel, grid=(rows // ROWS,), out_shape=jax.ShapeDty...  18.5 us
    squeeze x2, local copies, waits for them, and re-layouts, body(): return (solved[0], solved[1])  10.3 us
    dot_general x1, matrix products, body(): jnp.matmul(solve_matrix(block_inv, lower_mult), rhs, precision=lax.Precis...  9.98 us
    all_to_all x2, starting transfers between devices, spread(): return lax.all_to_all(field, 'gx', split_axis=1, concat_axis=1, tiled=True)  9.97 us
  transfers between devices with their start and end apart: 3, of which 3 were waited for; matrix products, arithmetic and copies ran while one was open for 3% of the time, Pallas kernels for 0%

profile of v1, /device:TPU:4, one launch (start us, length us, event | category | flops | bytes accessed | tf_op | source)
XLA Modules:
  0.0 407.4 jit_solution(13532245029733955253)
XLA Ops:
  0.6 0.0 copy-start
  0.6 3.7 copy.19
  4.4 3.7 all-to-all-start
  8.0 3.7 copy.20
  11.7 0.0 copy-start.8
  11.7 29.1 %all-to-all-done = f32[2,4,24,3840]{3,2,0,1:T(8,128)S(1)} async-done(((f32[2,4,24,3840]{3,2,0,1:T(8,128)}), f32[2,4,24,3840]{3,2,0,1:T(8,128)S(1)}, u32[]{:S(2)}, u32[]{:S(2)}) %all-to-all-start) | async-done | bytes 2949152 | tf_op jit(solution)/shard_map/all_to_all | solution.py:238
  40.8 0.0 copy-start.6
  40.8 1.6 copy-done.6
  42.4 6.3 %all-to-all-start.1 = ((f32[2,4,24,3840]{3,2,0,1:T(8,128)}), f32[2,4,24,3840]{3,2,0,1:T(8,128)}, u32[]{:S(2)}, u32[]{:S(2)}) async-start(f32[2,4,24,3840]{3,2,0,1:T(8,128)} %copy.20), calls=%async_computation.1 | async-start | bytes 5898240 | tf_op jit(solution)/shard_map/all_to_all | solution.py:238
  48.7 0.0 copy-done.8
  48.7 2.0 copy.21.a_ref
  50.8 0.0 copy-start.5
  50.8 31.2 %all-to-all-done.1 = f32[2,4,24,3840]{3,2,0,1:T(8,128)} async-done(((f32[2,4,24,3840]{3,2,0,1:T(8,128)}), f32[2,4,24,3840]{3,2,0,1:T(8,128)}, u32[]{:S(2)}, u32[]{:S(2)}) %all-to-all-start.1) | async-done | bytes 2949152 | tf_op jit(solution)/shard_map/all_to_all | solution.py:238
  82.0 0.0 copy-start.3
  82.0 0.0 copy-start.4
  82.0 2.1 copy.22.b_ref
  84.1 0.0 copy-done.5
  84.1 0.0 copy-done.3
  84.1 0.0 copy-done.4
  84.1 18.5 %shard_map.95 = f32[2,2,2,4,24,1920]{5,4,3,2,1,0:T(8,128)S(1)} custom-call(f32[2,4,24,3840]{3,2,1,0:T(8,128)S(1)} %copy.21.a_ref, f32[2,4,24,3840]{3,2,1,0:T(8,128)S(1)} %copy.22.b_ref, f32[1,3840]{1,0:T(1,128)S(1)} %reshape.34.keep_ref, f32[2,45,128]{2,1,0:T(8,128)S(1)} %copy-done.5, bf16[2,256,256]{2,1,0:T(8,128)(2,1)S(1)} %copy-done.3, ...), custom_call_target="tpu_custom_call" | custom-call | flops 6794772480 | bytes 6291456 | tf_op jit(solution)/shard_map/pallas_call | solution.py:186
  102.7 0.0 copy-start.2
  102.7 2.6 copy-done.2
  105.2 7.2 %all-to-all-start.2 = ((f32[32,24,1920]{2,1,0:T(8,128)}), f32[32,24,1920]{2,1,0:T(8,128)}, u32[]{:S(2)}, u32[]{:S(2)}) async-start(f32[32,24,1920]{2,1,0:T(8,128)} %bitcast.144), calls=%async_computation.2 | async-start | bytes 11796480 | tf_op jit(solution)/shard_map/all_to_all | solution.py:247
  112.4 0.0 copy-start.7
  112.4 0.3 iota_compare_fusion
  112.8 0.6 copy-done.7
  113.4 0.3 bitcast_dynamic-update-slice_fusion.3
  113.7 0.5 bitcast_dynamic-update-slice_fusion.2
  114.2 0.5 bitcast_dynamic-update-slice_fusion.1
  114.7 0.5 bitcast_dynamic-update-slice_fusion
  115.2 0.5 fusion.8
  115.7 0.0 copy-done
  115.7 2.2 convolution_bitcast_fusion
  118.0 0.5 fusion.5
  118.5 0.5 fusion.4
  119.0 0.5 fusion.3
  119.6 0.5 fusion.2
  120.1 0.5 fusion.1
  120.8 121.6 %all-to-all-done.2 = f32[32,24,1920]{2,1,0:T(8,128)} async-done(((f32[32,24,1920]{2,1,0:T(8,128)}), f32[32,24,1920]{2,1,0:T(8,128)}, u32[]{:S(2)}, u32[]{:S(2)}) %all-to-all-start.2) | async-done | bytes 5898272 | tf_op jit(solution)/shard_map/all_to_all | solution.py:247
  242.4 10.0 %fusion.38 = f32[8,96,1920]{2,1,0:T(8,128)S(1)} fusion(f32[8,96,768]{2,1,0:T(8,128)S(1)} %bitcast.146, f32[768,1920,1]{1,0,2:T(8,128)} %bitcast.33), kind=kOutput, calls=%fused_computation.65 | convolution fusion | flops 6794772480 | bytes 14155776 | tf_op jit(solution)/shard_map/dot_general | solution.py:249
  252.4 136.7 %all_to_all.20 = f32[8,96,1920]{2,1,0:T(8,128)S(1)} all-to-all(f32[8,96,1920]{2,1,0:T(8,128)S(1)} %fusion.38), channel_id=1, replica_groups=mesh['wa'=8,'gx'=4] {'wa'}, dimensions={0} | all-to-all | bytes 11796480 | tf_op jit(solution)/shard_map/all_to_all | solution.py:252
  389.0 0.4 fusion.37
  389.4 3.9 copy.23
  393.3 5.1 %squeeze.61 = f32[2,1,96,3840]{3,2,1,0:T(8,128)} reshape(f32[1,2,96,2,1920]{4,3,2,1,0:T(2,128)} %copy.23) | data formatting | bytes 5898240 | tf_op jit(solution)/shard_map/squeeze | solution.py:255
  398.4 0.0 copy-start.1
  398.4 3.9 copy.24
  402.3 5.1 %squeeze.62 = f32[2,1,96,3840]{3,2,1,0:T(8,128)} reshape(f32[1,2,96,2,1920]{4,3,2,1,0:T(2,128)} %copy.24) | data formatting | bytes 5898240 | tf_op jit(solution)/shard_map/squeeze | solution.py:255
  407.4 0.0 copy-done.1
  (8 shorter events, 0.2 us)
Async XLA Ops:
  0.6 115.1 %copy-start = (f32[6,128,128]{2,1,0:T(8,128)S(1)}, f32[6,128,128]{2,1,0:T(8,128)}, u32[]{:S(2)}) copy-start(f32[6,128,128]{2,1,0:T(8,128)} %param.11) | copy-start | bytes 1179652
  4.4 36.5 %all-to-all-start = ((f32[2,4,24,3840]{3,2,0,1:T(8,128)}), f32[2,4,24,3840]{3,2,0,1:T(8,128)S(1)}, u32[]{:S(2)}, u32[]{:S(2)}) async-start(f32[2,4,24,3840]{3,2,0,1:T(8,128)} %copy.19), calls=%async_computation | async-start | bytes 5898240 | tf_op jit(solution)/shard_map/all_to_all | solution.py:238
  11.7 37.0 %copy-start.8 = (s32[3840]{0:T(1024)S(1)}, s32[3840]{0:T(1024)}, u32[]{:S(2)}) copy-start(s32[3840]{0:T(1024)} %param.10) | copy-start | bytes 46084
  40.8 1.6 copy-start.6
  42.4 39.6 %all-to-all-start.1 = ((f32[2,4,24,3840]{3,2,0,1:T(8,128)}), f32[2,4,24,3840]{3,2,0,1:T(8,128)}, u32[]{:S(2)}, u32[]{:S(2)}) async-start(f32[2,4,24,3840]{3,2,0,1:T(8,128)} %copy.20), calls=%async_computation.1 | async-start | bytes 5898240 | tf_op jit(solution)/shard_map/all_to_all | solution.py:238
  50.8 33.3 %copy-start.5 = (f32[2,45,128]{2,1,0:T(8,128)S(1)}, f32[2,45,128]{2,1,0:T(8,128)}, u32[]{:S(2)}) copy-start(f32[2,45,128]{2,1,0:T(8,128)} %constant.6.clone.twist_ref) | copy-start | bytes 138244
  82.0 2.1 copy-start.3
  82.0 2.1 copy-start.4
  102.7 2.6 copy-start.2
  105.2 137.1 %all-to-all-start.2 = ((f32[32,24,1920]{2,1,0:T(8,128)}), f32[32,24,1920]{2,1,0:T(8,128)}, u32[]{:S(2)}, u32[]{:S(2)}) async-start(f32[32,24,1920]{2,1,0:T(8,128)} %bitcast.144), calls=%async_computation.2 | async-start | bytes 11796480 | tf_op jit(solution)/shard_map/all_to_all | solution.py:247
  112.4 1.0 copy-start.7
  398.4 9.0 %copy-start.1 = (f32[6,128,128]{2,1,0:T(8,128)S(1)}, f32[6,128,128]{2,1,0:T(8,128)}, u32[]{:S(2)}) copy-start(f32[6,128,128]{2,1,0:T(8,128)} %param.11) | copy-start | bytes 1179652

commit v2 on v1

--- a/solution.py
+++ b/solution.py
@@ -151,12 +151,9 @@
             cols = pl.ds(t * LANES, LANES)
             keep = keep_ref[:, cols]
             ins = [(hat_ref[x, f, t, 0], hat_ref[x, f, t, 1]) for x in range(KXT)]
-            into = pl.ds(t % half * LANES, LANES)
             for k, value in enumerate(dft4(ins, -1)):
                 for part in range(2):
-                    out_ref[f, part, t // half, k, :, into] = (
-                        ref[part, k, :, cols] + value[part] * keep
-                    )
+                    out_ref[f, part, k, :, cols] = ref[part, k, :, cols] + value[part] * keep
 
 
 def front_tables(modes):
@@ -186,7 +183,7 @@
     return pl.pallas_call(
         front_kernel,
         grid=(rows // ROWS,),
-        out_shape=jax.ShapeDtypeStruct((2, 2, 2, KXT, rows, modes // 2), jnp.float32),
+        out_shape=jax.ShapeDtypeStruct((2, 2, KXT, rows, modes), jnp.float32),
         in_specs=[
             field_spec,
             field_spec,
@@ -195,7 +192,7 @@
             pl.BlockSpec(inv.shape, lambda i: (0, 0, 0)),
             pl.BlockSpec(fwd.shape, lambda i: (0, 0, 0)),
         ],
-        out_specs=pl.BlockSpec((2, 2, 2, KXT, ROWS, modes // 2), lambda i: (0, 0, 0, 0, i, 0)),
+        out_specs=pl.BlockSpec((2, 2, KXT, ROWS, modes), lambda i: (0, 0, 0, i, 0)),
         scratch_shapes=[
             pltpu.VMEM((KXT, 2, 30, 2, ROWS, LANES), jnp.float32),
             pltpu.VMEM((5, 9, 2, ROWS, LANES), jnp.float32),
@@ -224,6 +221,164 @@
     return jnp.concatenate(solved, axis=0)
 
 
+def remote(src, dst, send_sem, recv_sem, wa, gx):
+    return pltpu.make_async_remote_copy(
+        src_ref=src, dst_ref=dst, send_sem=send_sem, recv_sem=recv_sem,
+        device_id=(wa, gx), device_id_type=pl.DeviceIdType.MESH,
+    )
+
+
+def solve_kernel(chunks, group, gx_size, rhs_ref, up_ref, full_ref, out_ref,
+                 held, solved, msg_out, msg_in,
+                 send_sem, recv_sem, own_sem, msg_send, msg_recv, back_send, back_recv, back_own):
+    wa, gx = lax.axis_index("wa"), lax.axis_index("gx")
+    lane_count = rhs_ref.shape[-1] // chunks
+    rows = out_ref.shape[1]
+    base, spot = wa // group * group, wa % group
+    partner = (wa + group) % (2 * group)
+    count = group * gx_size
+    me = spot * gx_size + gx
+    barrier = pltpu.get_barrier_semaphore()
+    for k in range(1, count):
+        peer = (me + k) % count
+        pl.semaphore_signal(barrier, inc=1, device_id=(base + peer // gx_size, peer % gx_size),
+                            device_id_type=pl.DeviceIdType.MESH)
+    pl.semaphore_signal(barrier, inc=1, device_id=(partner, gx),
+                        device_id_type=pl.DeviceIdType.MESH)
+    pl.semaphore_wait(barrier, count)
+
+    def columns(c):
+        return pl.ds(pl.multiple_of(c * lane_count, LANES), lane_count)
+
+    def piece_to(c, k):
+        peer = (me + k) % count
+        return remote(rhs_ref.at[peer, :, columns(c)], held.at[me, :, columns(c)],
+                      send_sem.at[c, k], recv_sem.at[c, k], base + peer // gx_size, peer % gx_size)
+
+    def piece_from(c, k):
+        peer = (me + count - k) % count
+        return remote(rhs_ref.at[peer, :, columns(c)], held.at[peer, :, columns(c)],
+                      send_sem.at[c, k], recv_sem.at[c, k], base + peer // gx_size, peer % gx_size)
+
+    def own_piece(c):
+        return pltpu.make_async_copy(rhs_ref.at[me, :, columns(c)], held.at[me, :, columns(c)],
+                                     own_sem.at[c])
+
+    def message(c):
+        return remote(msg_out.at[:, columns(c)], msg_in.at[:, columns(c)],
+                      msg_send.at[c], msg_recv.at[c], partner, gx)
+
+    def back_to(c, k):
+        peer = (spot + k) % group
+        return remote(solved.at[peer, :, columns(c)], out_ref.at[spot, :, columns(c)],
+                      back_send.at[c, k], back_recv.at[c, k], base + peer, gx)
+
+    def back_from(c, k):
+        peer = (spot + group - k) % group
+        return remote(solved.at[peer, :, columns(c)], out_ref.at[peer, :, columns(c)],
+                      back_send.at[c, k], back_recv.at[c, k], base + peer, gx)
+
+    def back_own_piece(c):
+        return pltpu.make_async_copy(solved.at[spot, :, columns(c)], out_ref.at[spot, :, columns(c)],
+                                     back_own.at[c])
+
+    def gathered(c):
+        return held[:, :, columns(c)].reshape(group * rows, lane_count)
+
+    def start_pieces(c, carry):
+        own_piece(c).start()
+        for k in range(1, count):
+            piece_to(c, k).start()
+        return carry
+
+    def send_message(c, carry):
+        own_piece(c).wait()
+        for k in range(1, count):
+            piece_from(c, k).wait_recv()
+        msg_out[:, columns(c)] = split_matmul(up_ref[...], gathered(c))
+        message(c).start()
+        return carry
+
+    def finish(c, carry):
+        message(c).wait_recv()
+        vectors = jnp.concatenate([gathered(c), msg_in[:, columns(c)]], axis=0)
+        result = split_matmul(full_ref[...], vectors)
+        solved[:, :, columns(c)] = result.reshape(group, rows, lane_count)
+        back_own_piece(c).start()
+        for k in range(1, group):
+            back_to(c, k).start()
+        return carry
+
+    def drain(c, carry):
+        for k in range(1, count):
+            piece_to(c, k).wait_send()
+        message(c).wait_send()
+        back_own_piece(c).wait()
+        for k in range(1, group):
+            back_to(c, k).wait_send()
+            back_from(c, k).wait_recv()
+        return carry
+
+    for step in (start_pieces, send_message, finish, drain):
+        lax.fori_loop(0, chunks, step, 0)
+
+
+def split_matmul(left, right):
+    l_hi, r_hi = left.astype(jnp.bfloat16), right.astype(jnp.bfloat16)
+    l_lo = (left - l_hi.astype(jnp.float32)).astype(jnp.bfloat16)
+    r_lo = (right - r_hi.astype(jnp.float32)).astype(jnp.bfloat16)
+    dot = functools.partial(jnp.dot, preferred_element_type=jnp.float32)
+    return dot(l_hi, r_hi) + (dot(l_lo, r_hi) + dot(l_hi, r_lo))
+
+
+def solve_across(wa, gx, rhs, block_inv, lower_mult):
+    share, modes = rhs.shape[-2:]
+    group = wa // 2
+    count, width = group * gx, block_inv.shape[1]
+    rows = share * gx
+    half = group * rows
+    middle = half // width
+    dot = functools.partial(jnp.matmul, precision=lax.Precision.HIGHEST)
+    dense = solve_matrix(block_inv, lower_mult)
+    eye = jnp.eye(width, dtype=jnp.float32)
+    state, answer = [eye], [-lower_mult[middle - 1].T]
+    for j in range(middle - 2, -1, -1):
+        state.insert(0, -dot(state[0], lower_mult[j]))
+        answer.insert(0, -dot(lower_mult[j].T, answer[0]))
+    low = lax.axis_index("wa") < group
+    up = jnp.where(low, jnp.concatenate(state, axis=1), dense[half : half + width, half:])
+    diagonal = jnp.where(low, dense[:half, :half], dense[half:, half:])
+    side = jnp.where(low, jnp.concatenate(answer, axis=0), dense[half:, half - width : half])
+    full = jnp.concatenate([diagonal, side], axis=1)
+    chunks = 5
+    dma = pltpu.SemaphoreType.DMA
+    vmem = pl.BlockSpec(memory_space=pltpu.VMEM)
+    anywhere = pl.BlockSpec(memory_space=pl.ANY)
+    return pl.pallas_call(
+        functools.partial(solve_kernel, chunks, group, gx),
+        out_shape=jax.ShapeDtypeStruct((group, rows, modes), jnp.float32),
+        in_specs=[anywhere, vmem, vmem],
+        out_specs=anywhere,
+        scratch_shapes=[
+            pltpu.VMEM((count, share, modes), jnp.float32),
+            pltpu.VMEM((group, rows, modes), jnp.float32),
+            pltpu.VMEM((width, modes), jnp.float32),
+            pltpu.VMEM((width, modes), jnp.float32),
+            dma((chunks, count)),
+            dma((chunks, count)),
+            dma((chunks,)),
+            dma((chunks,)),
+            dma((chunks,)),
+            dma((chunks, group)),
+            dma((chunks, group)),
+            dma((chunks,)),
+        ],
+        compiler_params=pltpu.CompilerParams(
+            vmem_limit_bytes=40 * 1024 * 1024, collective_id=0, has_side_effects=True
+        ),
+    )(rhs.reshape(count, share, modes), up, full)
+
+
 def body(wa, gx, field_a, field_b, keep_mask, block_inv, lower_mult):
     _, _, rows, modes = field_a.shape
     keep = keep_mask.astype(jnp.float32).reshape(1, modes)
@@ -238,11 +393,13 @@
         return lax.all_to_all(field, "gx", split_axis=1, concat_axis=1, tiled=True)
 
     rhs = front(spread(field_a), spread(field_b), keep)
+    if wa == 8 and gx == KXT and rows == padded and rows * 4 % block_inv.shape[1] == 0:
+        solved = solve_across(wa, gx, rhs, block_inv, lower_mult)
+        solved = solved.reshape(2, 2, 1, rows, modes)
+        return (solved[0], solved[1])
     chunks = wa // 4
     width = modes // chunks
-    if chunks != 2:
-        rhs = jnp.moveaxis(rhs, 2, 4).reshape(2, 2, KXT, share, chunks, width)
-        rhs = jnp.moveaxis(rhs, 4, 2)
+    rhs = jnp.moveaxis(rhs.reshape(2, 2, KXT, share, chunks, width), 4, 2)
     rhs = rhs.reshape(wa * gx, share, width)
     rhs = lax.all_to_all(rhs, ("wa", "gx"), split_axis=0, concat_axis=0, tiled=True)
     rhs = rhs.reshape(wa, padded, width)[:, :rows].reshape(wa * rows, width)

time: 408 us -> 295 us (0.72)
  Pallas kernels: 18.5 us -> 204 us
  waiting for transfers between devices: 182 us -> 36.5 us
  blocking collectives: 137 us -> 0 us
  local copies, waits for them, and re-layouts: 34.9 us -> 18.4 us
  starting transfers between devices: 17.1 us -> 11.5 us
  other arithmetic: 0.33 us -> 4.91 us
    pallas_call x0 -> x1, Pallas kernels: none -> 186 us  [solve_across(): pl.pallas_call(functools.partial(solve_kernel, chunks, group, gx), out_sh...]
    all_to_all x1 -> x0, blocking collectives: 137 us -> none  [body(): lax.all_to_all(solved, 'wa', split_axis=0, concat_axis=0, tiled=True)]
    all_to_all x1 -> x0, waiting for transfers between devices: 122 us -> none  [body(): lax.all_to_all(rhs, ('wa', 'gx'), split_axis=0, concat_axis=0, tiled=True)]
    all_to_all x2, waiting for transfers between devices: 60.3 us -> 36.5 us  [spread(): return lax.all_to_all(field, 'gx', split_axis=1, concat_axis=1, tiled=True)]
    squeeze x2 -> x1, local copies, waits for them, and re-layouts: 10.3 us -> 0.78 us  [solve_matrix(): solved = [own[-1]]]
    dot_general x1 -> x4, matrix products: 9.98 us -> 1.6 us  [the longest x2 1.21 us: solve_across(): answer.insert(0, -dot(lower_mult[j].T, answer[0]))]
    slice x3 -> x2, local copies, waits for them, and re-layouts: 8.11 us -> 0.01 us  [solve_matrix(): reduced.append(eye[j] - dot(lower_mult[j - 1], reduced[-1]))]
    all_to_all x1 -> x0, starting transfers between devices: 7.18 us -> none  [body(): lax.all_to_all(rhs, ('wa', 'gx'), split_axis=0, concat_axis=0, tiled=True)]
  transfers between devices with their start and end apart: 3 -> 2, of which waited for: 3 -> 2; matrix products, arithmetic and copies ran while one was open for 3% -> 10% of each run, Pallas kernels for 0% -> 0%
where the time goes in v2:
time: 295 us; the launch traced here: 291 us
  Pallas kernels  204 us (69%)
  waiting for transfers between devices  36.5 us (12%)
  local copies, waits for them, and re-layouts  18.4 us (6%)
  matrix products  14.9 us (5%)
  starting transfers between devices  11.5 us (4%)
  other arithmetic  4.91 us (2%)
    pallas_call x1, Pallas kernels, solve_across(): pl.pallas_call(functools.partial(solve_kernel, chunks, group, gx), out_sh...  186 us
    all_to_all x2, waiting for transfers between devices, spread(): return lax.all_to_all(field, 'gx', split_axis=1, concat_axis=1, tiled=True)  36.5 us
    pallas_call x1, Pallas kernels, front(): pl.pallas_call(front_kernel, grid=(rows // ROWS,), out_shape=jax.ShapeDty...  18.5 us
    all_to_all x2, starting transfers between devices, spread(): return lax.all_to_all(field, 'gx', split_axis=1, concat_axis=1, tiled=True)  11.5 us
    another operation x2, local copies, waits for them, and re-layouts, spread(): field = field.reshape(2, gx, share, modes)  7.4 us
    dot_general x5, matrix products, solve_matrix(): reduced.append(eye[j] - dot(lower_mult[j - 1], reduced[-1]))  6.85 us
  transfers between devices with their start and end apart: 2, of which 2 were waited for; matrix products, arithmetic and copies ran while one was open for 10% of the time, Pallas kernels for 0%

profile of v2, /device:TPU:4, one launch (start us, length us, event | category | flops | bytes accessed | tf_op | source)
XLA Modules:
  0.0 291.4 jit_solution(5347920598066581737)
XLA Ops:
  0.6 0.0 copy-start
  0.6 3.7 %copy.24 = f32[2,4,24,3840]{3,2,0,1:T(8,128)} copy(f32[2,4,24,3840]{3,2,1,0:T(8,128)} %bitcast.160) | data formatting | bytes 5898240 | tf_op jit(solution)/shard_map/reshape;reshape | solution.py:392
  4.4 4.6 %all-to-all-start = ((f32[2,4,24,3840]{3,2,0,1:T(8,128)}), f32[2,4,24,3840]{3,2,0,1:T(8,128)}, u32[]{:S(2)}, u32[]{:S(2)}) async-start(f32[2,4,24,3840]{3,2,0,1:T(8,128)} %copy.24), calls=%async_computation | async-start | bytes 5898240 | tf_op jit(solution)/shard_map/all_to_all | solution.py:393
  9.0 0.0 slice-start
  9.0 0.0 copy-start.5
  9.0 1.1 iota_compare_fusion
  10.1 0.8 fusion.14
  10.9 0.0 slice-done
  10.9 0.1 copy.37
  11.0 0.0 copy-done.5
  11.0 0.0 copy-start.9
  11.0 0.3 convolution_negate_fusion.1
  11.3 0.0 copy-start.8
  11.3 0.9 fusion.12
  12.2 0.0 copy-done.9
  12.2 1.9 bitcast_dynamic-update-slice_fusion.3
  14.1 1.5 fusion.31
  15.6 0.0 copy-start.10
  15.6 3.7 %copy.25 = f32[2,4,24,3840]{3,2,0,1:T(8,128)} copy(f32[2,4,24,3840]{3,2,1,0:T(8,128)} %bitcast.161) | data formatting | bytes 5898240 | tf_op jit(solution)/shard_map/reshape;reshape | solution.py:392
  19.3 0.0 copy-done.8
  19.3 0.0 copy-done.10
  19.3 1.2 bitcast_dynamic-update-slice_fusion.2
  20.5 1.2 bitcast_dynamic-update-slice_fusion.1
  21.8 1.3 bitcast_dynamic-update-slice_fusion
  23.0 1.2 fusion.7
  24.3 0.0 copy-done
  24.3 0.0 copy-start.6
  24.3 3.9 %convolution_bitcast_fusion = f32[6,128,768]{2,1,0:T(8,128)S(1)} fusion(f32[6,128,768]{1,2,0:T(8,128)} %fusion.7, f32[6,128,128]{2,1,0:T(8,128)S(1)} %copy-done), kind=kOutput, calls=%fused_computation.3 | convolution fusion | flops 905969664 | bytes 5111808 | tf_op jit(solution)/shard_map/dot_general | solution.py:217
  28.2 0.8 slice_bitcast_fusion.5
  29.0 0.0 copy-done.6
  29.0 0.5 fusion.4
  29.5 0.5 fusion.3
  30.1 11.2 %all-to-all-done = f32[2,4,24,3840]{3,2,0,1:T(8,128)} async-done(((f32[2,4,24,3840]{3,2,0,1:T(8,128)}), f32[2,4,24,3840]{3,2,0,1:T(8,128)}, u32[]{:S(2)}, u32[]{:S(2)}) %all-to-all-start) | async-done | bytes 2949152 | tf_op jit(solution)/shard_map/all_to_all | solution.py:393
  41.3 6.9 %all-to-all-start.1 = ((f32[2,4,24,3840]{3,2,0,1:T(8,128)}), f32[2,4,24,3840]{3,2,0,1:T(8,128)}, u32[]{:S(2)}, u32[]{:S(2)}) async-start(f32[2,4,24,3840]{3,2,0,1:T(8,128)} %copy.25), calls=%async_computation.1 | async-start | bytes 5898240 | tf_op jit(solution)/shard_map/all_to_all | solution.py:393
  48.1 0.0 copy-start.7
  48.1 1.0 maximum_select_fusion
  49.2 1.1 pad_maximum_fusion
  50.2 0.0 copy-done.7
  50.2 0.5 fusion.2
  50.8 0.5 fusion.1
  51.3 0.5 fusion
  51.8 0.1 slice_select_fusion
  51.9 0.1 pad_maximum_fusion.1.full_ref
  52.0 0.2 convolution_negate_fusion.3
  52.2 0.2 convolution_negate_fusion.2
  52.4 3.6 %copy.26.a_ref = f32[2,4,24,3840]{3,2,1,0:T(8,128)} copy(f32[2,4,24,3840]{3,2,0,1:T(8,128)} %all-to-all-done) | data formatting | bytes 5898240 | tf_op jit(solution)/shard_map/all_to_all | solution.py:393
  56.1 0.0 copy-start.2
  56.1 0.0 copy-start.3
  56.1 0.0 copy-start.4
  56.1 25.3 %all-to-all-done.1 = f32[2,4,24,3840]{3,2,0,1:T(8,128)} async-done(((f32[2,4,24,3840]{3,2,0,1:T(8,128)}), f32[2,4,24,3840]{3,2,0,1:T(8,128)}, u32[]{:S(2)}, u32[]{:S(2)}) %all-to-all-start.1) | async-done | bytes 2949152 | tf_op jit(solution)/shard_map/all_to_all | solution.py:393
  81.4 0.0 copy-start.1
  81.4 2.2 copy.27.b_ref
  83.6 0.0 copy-done.2
  83.6 0.0 copy-done.3
  83.6 0.0 copy-done.4
  83.6 0.5 copy-done.1
  84.1 18.5 %shard_map.95 = f32[2,2,4,24,3840]{4,3,2,1,0:T(8,128)S(1)} custom-call(f32[2,4,24,3840]{3,2,1,0:T(8,128)S(1)} %copy-done.1, f32[2,4,24,3840]{3,2,1,0:T(8,128)S(1)} %copy.27.b_ref, f32[1,3840]{1,0:T(1,128)S(1)} %reshape.29.keep_ref, f32[2,45,128]{2,1,0:T(8,128)S(1)} %copy-done.4, bf16[2,256,256]{2,1,0:T(8,128)(2,1)S(1)} %copy-done.2, ...), custom_call_target="tpu_custom_call" | custom-call | flops 6794772480 | bytes 6291456 | tf_op jit(solution)/shard_map/pallas_call | solution.py:183
  102.7 185.8 %shard_map.96 = f32[4,96,3840]{2,1,0:T(8,128)S(1)} custom-call(f32[16,24,3840]{2,1,0:T(8,128)S(1)} %bitcast.159, f32[128,384]{1,0:T(8,128)S(1)} %slice_select_fusion.1.up_ref, f32[384,512]{1,0:T(8,128)S(1)} %pad_maximum_fusion.1.full_ref), custom_call_target="tpu_custom_call" | custom-call | tf_op jit(solution)/shard_map/pallas_call | solution.py:357
  288.5 3.0 %slice_bitcast_fusion = (f32[2,1,96,3840]{3,2,1,0:T(8,128)}, f32[2,1,96,3840]{3,2,1,0:T(8,128)}) fusion(f32[4,96,3840]{2,1,0:T(8,128)S(1)} %shard_map.96), kind=kLoop, calls=%fused_computation | loop fusion | bytes 11796480
  (4 shorter events, 0.1 us)
Async XLA Ops:
  0.6 23.7 %copy-start = (f32[6,128,128]{2,1,0:T(8,128)S(1)}, f32[6,128,128]{2,1,0:T(8,128)}, u32[]{:S(2)}) copy-start(f32[6,128,128]{2,1,0:T(8,128)} %param.11) | copy-start | bytes 1179652
  4.4 36.9 %all-to-all-start = ((f32[2,4,24,3840]{3,2,0,1:T(8,128)}), f32[2,4,24,3840]{3,2,0,1:T(8,128)}, u32[]{:S(2)}, u32[]{:S(2)}) async-start(f32[2,4,24,3840]{3,2,0,1:T(8,128)} %copy.24), calls=%async_computation | async-start | bytes 5898240 | tf_op jit(solution)/shard_map/all_to_all | solution.py:393
  9.0 1.9 slice-start
  9.0 2.0 copy-start.5
  11.0 1.2 copy-start.9
  11.3 8.0 %copy-start.8 = (f32[128,128]{1,0:T(8,128)}, f32[128,128]{1,0:T(8,128)S(1)}, u32[]{:S(2)}) copy-start(f32[128,128]{1,0:T(8,128)S(1)} %convolution_negate_fusion.1) | copy-start | bytes 196612
  15.6 3.7 %copy-start.10 = (s32[3840]{0:T(1024)S(1)}, s32[3840]{0:T(1024)}, u32[]{:S(2)}) copy-start(s32[3840]{0:T(1024)} %param.10) | copy-start | bytes 46084
  24.3 4.7 %copy-start.6 = (f32[5,128,128]{2,1,0:T(8,128)S(1)}, f32[5,128,128]{2,1,0:T(8,128)}, u32[]{:S(2)}) copy-start(f32[5,128,128]{2,1,0:T(8,128)} %param.12) | copy-start | bytes 983044
  41.3 40.1 %all-to-all-start.1 = ((f32[2,4,24,3840]{3,2,0,1:T(8,128)}), f32[2,4,24,3840]{3,2,0,1:T(8,128)}, u32[]{:S(2)}, u32[]{:S(2)}) async-start(f32[2,4,24,3840]{3,2,0,1:T(8,128)} %copy.25), calls=%async_computation.1 | async-start | bytes 5898240 | tf_op jit(solution)/shard_map/all_to_all | solution.py:393
  48.1 2.1 copy-start.7
  56.1 27.5 %copy-start.2 = (bf16[2,256,256]{2,1,0:T(8,128)(2,1)S(1)}, bf16[2,256,256]{2,1,0:T(8,128)(2,1)}, u32[]{:S(2)}) copy-start(bf16[2,256,256]{2,1,0:T(8,128)(2,1)} %constant.15.clone.winv_ref) | copy-start | bytes 786436
  56.1 27.5 %copy-start.3 = (bf16[2,256,256]{2,1,0:T(8,128)(2,1)S(1)}, bf16[2,256,256]{2,1,0:T(8,128)(2,1)}, u32[]{:S(2)}) copy-start(bf16[2,256,256]{2,1,0:T(8,128)(2,1)} %constant.16.clone.wfwd_ref) | copy-start | bytes 786436
  56.1 27.5 %copy-start.4 = (f32[2,45,128]{2,1,0:T(8,128)S(1)}, f32[2,45,128]{2,1,0:T(8,128)}, u32[]{:S(2)}) copy-start(f32[2,45,128]{2,1,0:T(8,128)} %constant.14.clone.twist_ref) | copy-start | bytes 138244
  81.4 2.7 copy-start.1

commit v3 on v1

--- a/solution.py
+++ b/solution.py
@@ -151,12 +151,9 @@
             cols = pl.ds(t * LANES, LANES)
             keep = keep_ref[:, cols]
             ins = [(hat_ref[x, f, t, 0], hat_ref[x, f, t, 1]) for x in range(KXT)]
-            into = pl.ds(t % half * LANES, LANES)
             for k, value in enumerate(dft4(ins, -1)):
                 for part in range(2):
-                    out_ref[f, part, t // half, k, :, into] = (
-                        ref[part, k, :, cols] + value[part] * keep
-                    )
+                    out_ref[f, part, k, :, cols] = ref[part, k, :, cols] + value[part] * keep
 
 
 def front_tables(modes):
@@ -186,7 +183,7 @@
     return pl.pallas_call(
         front_kernel,
         grid=(rows // ROWS,),
-        out_shape=jax.ShapeDtypeStruct((2, 2, 2, KXT, rows, modes // 2), jnp.float32),
+        out_shape=jax.ShapeDtypeStruct((2, 2, KXT, rows, modes), jnp.float32),
         in_specs=[
             field_spec,
             field_spec,
@@ -195,7 +192,7 @@
             pl.BlockSpec(inv.shape, lambda i: (0, 0, 0)),
             pl.BlockSpec(fwd.shape, lambda i: (0, 0, 0)),
         ],
-        out_specs=pl.BlockSpec((2, 2, 2, KXT, ROWS, modes // 2), lambda i: (0, 0, 0, 0, i, 0)),
+        out_specs=pl.BlockSpec((2, 2, KXT, ROWS, modes), lambda i: (0, 0, 0, i, 0)),
         scratch_shapes=[
             pltpu.VMEM((KXT, 2, 30, 2, ROWS, LANES), jnp.float32),
             pltpu.VMEM((5, 9, 2, ROWS, LANES), jnp.float32),
@@ -210,18 +207,259 @@
     )(slab_a, slab_b, keep, jnp.asarray(twist), jnp.asarray(inv), jnp.asarray(fwd))
 
 
-def solve_matrix(block_inv, lower_mult):
+def solve_matrices(block_inv, lower_mult):
     count, width = block_inv.shape[:2]
     dot = functools.partial(jnp.matmul, precision=lax.Precision.HIGHEST)
     eye = jnp.eye(count * width, dtype=jnp.float32).reshape(count, width, count * width)
     reduced = [eye[0]]
     for j in range(1, count):
         reduced.append(eye[j] - dot(lower_mult[j - 1], reduced[-1]))
-    own = dot(block_inv, jnp.stack(reduced))
-    solved = [own[-1]]
+    back = [eye[-1]]
     for j in range(count - 2, -1, -1):
-        solved.insert(0, own[j] - dot(lower_mult[j].T, solved[0]))
-    return jnp.concatenate(solved, axis=0)
+        back.insert(0, eye[j] - dot(lower_mult[j].T, back[0]))
+    reduced = jnp.stack(reduced)
+    back = jnp.concatenate(back, axis=0)
+    dense = dot(back, dot(block_inv, reduced).reshape(count * width, count * width))
+    return reduced.reshape(count * width, count * width), back, dense
+
+
+def remote(src, dst, send_sem, recv_sem, wa, gx):
+    return pltpu.make_async_remote_copy(
+        src_ref=src, dst_ref=dst, send_sem=send_sem, recv_sem=recv_sem,
+        device_id=(wa, gx), device_id_type=pl.DeviceIdType.MESH,
+    )
+
+
+def solve_kernel(chunks, planes, per_plane, gx_size, rhs_ref, local_ref, step_ref, full_ref, out_ref,
+                 held, solved, near_out, near_in, far_out, far_in,
+                 send_sem, recv_sem, own_sem, near_send, near_recv, far_send, far_recv,
+                 back_send, back_recv, back_own):
+    wa, gx = lax.axis_index("wa"), lax.axis_index("gx")
+    lanes = near_out.shape[-1]
+    rows = out_ref.shape[1]
+    parts = held.shape[0]
+    width = near_out.shape[1]
+    per_part = chunks // parts
+    z, x = wa // per_plane, wa % per_plane
+    count = per_plane * gx_size
+    me = x * gx_size + gx
+    base = z * per_plane
+    low = (z < planes // 2).astype(jnp.int32)
+    inner = wa + per_plane * (2 * low - 1)
+    outer = wa - per_plane * (2 * low - 1)
+    middle = jnp.logical_and(z > 0, z < planes - 1)
+    edge = jnp.logical_or(z == 0, z == planes - 1)
+    barrier = pltpu.get_barrier_semaphore()
+
+    def greet(to_wa, to_gx):
+        pl.semaphore_signal(barrier, inc=1, device_id=(to_wa, to_gx),
+                            device_id_type=pl.DeviceIdType.MESH)
+
+    for k in range(1, count):
+        peer = (me + k) % count
+        greet(base + peer // gx_size, peer % gx_size)
+    greet(inner, gx)
+
+    @pl.when(middle)
+    def _():
+        greet(outer, gx)
+
+    pl.semaphore_wait(barrier, count + middle.astype(jnp.int32))
+
+    def place(c):
+        return c // per_part, pl.ds(pl.multiple_of(c % per_part * lanes, LANES), lanes)
+
+    def piece(c, k, to):
+        part, cols = place(c)
+        peer = (me + k) % count if to else (me + count - k) % count
+        slot = me if to else peer
+        peer_x, peer_gx = peer // gx_size, peer % gx_size
+        return remote(rhs_ref.at[peer_x, part, peer_gx, :, cols], held.at[part, slot, :, cols],
+                      send_sem.at[c, k], recv_sem.at[c, k], base + peer_x, peer_gx)
+
+    def own_piece(c):
+        part, cols = place(c)
+        return pltpu.make_async_copy(rhs_ref.at[x, part, gx, :, cols], held.at[part, me, :, cols],
+                                     own_sem.at[c])
+
+    def near_from_edge(c, to):
+        return remote(near_out.at[c], near_in.at[c], near_send.at[c], near_recv.at[c], to, gx)
+
+    def near_from_middle(c):
+        return remote(near_out.at[c], far_in.at[c], near_send.at[c], far_recv.at[c], inner, gx)
+
+    def far_to_edge(c, to):
+        return remote(far_out.at[c], far_in.at[c], far_send.at[c], far_recv.at[c], to, gx)
+
+    def back(c, k, to):
+        part, cols = place(c)
+        peer = (x + k) % per_plane if to else (x + per_plane - k) % per_plane
+        slot = x if to else peer
+        return remote(solved.at[part, peer, :, cols], out_ref.at[slot * parts + part, :, cols],
+                      back_send.at[c, k], back_recv.at[c, k], base + peer, gx)
+
+    def back_own_piece(c):
+        part, cols = place(c)
+        return pltpu.make_async_copy(solved.at[part, x, :, cols],
+                                     out_ref.at[x * parts + part, :, cols], back_own.at[c])
+
+    def gathered(c):
+        part, cols = place(c)
+        return held[part, :, :, cols].reshape(per_plane * rows, lanes)
+
+    def start_pieces(c, carry):
+        own_piece(c).start()
+        for k in range(1, count):
+            piece(c, k, True).start()
+        return carry
+
+    def local_step(c):
+        own_piece(c).wait()
+        for k in range(1, count):
+            piece(c, k, False).wait_recv()
+        both = split_matmul(local_ref[...], gathered(c))
+        near_out[c] = both[:width]
+        far_out[c] = both[width:]
+
+        @pl.when(edge)
+        def _():
+            near_in[c] = jnp.zeros((width, lanes), jnp.float32)
+            near_from_edge(c, inner).start()
+
+    def near_step(c):
+        @pl.when(middle)
+        def _():
+            near_from_edge(c, outer).wait_recv()
+            near_out[c] = near_out[c] + split_matmul(step_ref[0], near_in[c])
+            near_from_middle(c).start()
+
+    def far_step(c):
+        @pl.when(middle)
+        def _():
+            near_from_middle(c).wait_recv()
+            far_out[c] = far_out[c] + split_matmul(step_ref[1], far_in[c])
+            far_to_edge(c, outer).start()
+
+    def finish(c):
+        @pl.when(edge)
+        def _():
+            far_to_edge(c, inner).wait_recv()
+
+        part, cols = place(c)
+        vectors = jnp.concatenate([gathered(c), near_in[c], far_in[c]], axis=0)
+        result = split_matmul(full_ref[...], vectors)
+        solved[part, :, :, cols] = result.reshape(per_plane, rows, lanes)
+        back_own_piece(c).start()
+        for k in range(1, per_plane):
+            back(c, k, True).start()
+
+    def drain(c, carry):
+        for k in range(1, count):
+            piece(c, k, True).wait_send()
+
+        @pl.when(edge)
+        def _():
+            near_from_edge(c, inner).wait_send()
+
+        @pl.when(middle)
+        def _():
+            near_from_middle(c).wait_send()
+            far_to_edge(c, outer).wait_send()
+
+        back_own_piece(c).wait()
+        for k in range(1, per_plane):
+            back(c, k, True).wait_send()
+            back(c, k, False).wait_recv()
+        return carry
+
+    lags = ((local_step, 0), (near_step, 2), (far_step, 4), (finish, 6))
+
+    def turn(t, carry):
+        for step, lag in lags:
+            c = t - lag
+
+            @pl.when(jnp.logical_and(c >= 0, c < chunks))
+            def _(step=step, c=c):
+                step(c)
+
+        return carry
+
+    lax.fori_loop(0, chunks, start_pieces, 0)
+    lax.fori_loop(0, chunks + lags[-1][1], turn, 0)
+    lax.fori_loop(0, chunks, drain, 0)
+
+
+def split_matmul(left, right):
+    l_hi, r_hi = left.astype(jnp.bfloat16), right.astype(jnp.bfloat16)
+    l_lo = (left - l_hi.astype(jnp.float32)).astype(jnp.bfloat16)
+    r_lo = (right - r_hi.astype(jnp.float32)).astype(jnp.bfloat16)
+    dot = functools.partial(jnp.dot, preferred_element_type=jnp.float32)
+    return dot(l_hi, r_hi) + (dot(l_lo, r_hi) + dot(l_hi, r_lo))
+
+
+def solve_across(wa, gx, rhs, block_inv, lower_mult):
+    share, modes = rhs.shape[-2:]
+    planes, per_plane, parts = 4, 2, 2
+    rows = share * gx
+    plane = per_plane * rows
+    count = per_plane * gx
+    nblocks, width = block_inv.shape[:2]
+    reduce_op, back_op, dense = solve_matrices(block_inv, lower_mult)
+    z = lax.axis_index("wa") // per_plane
+    first, after = z * plane, (z + 1) * plane
+    below = jnp.maximum(first - 1, 0) // width * width
+    start = first // width * width
+    end = (after - 1) // width * width
+    above = jnp.minimum(after, nblocks * width - 1) // width * width
+
+    def cut(table, row, height, column, span):
+        return lax.dynamic_slice(table, (row, column), (height, span))
+
+    up_local = cut(reduce_op, end, width, first, plane)
+    up_step = cut(reduce_op, end, width, below, width)
+    up_full = cut(dense, first, plane, below, width)
+    down_local = cut(dense, start, width, first, plane)
+    down_step = cut(back_op, start, width, above, width)
+    down_full = cut(back_op, first, plane, above, width)
+    low = z < planes // 2
+
+    def ordered(up, down, axis):
+        return jnp.where(low, jnp.concatenate([up, down], axis), jnp.concatenate([down, up], axis))
+
+    local = ordered(up_local, down_local, 0)
+    steps = ordered(up_step[None], down_step[None], 0)
+    full = jnp.concatenate([cut(dense, first, plane, first, plane),
+                            ordered(up_full, down_full, 1)], axis=1)
+    lanes = 6 * LANES
+    chunks = parts * modes // lanes
+    dma = pltpu.SemaphoreType.DMA
+    vmem = pl.BlockSpec(memory_space=pltpu.VMEM)
+    anywhere = pl.BlockSpec(memory_space=pl.ANY)
+    message = pltpu.VMEM((chunks, width, lanes), jnp.float32)
+    return pl.pallas_call(
+        functools.partial(solve_kernel, chunks, planes, per_plane, gx),
+        out_shape=jax.ShapeDtypeStruct((per_plane * parts, rows, modes), jnp.float32),
+        in_specs=[anywhere, vmem, vmem, vmem],
+        out_specs=anywhere,
+        scratch_shapes=[
+            pltpu.VMEM((parts, count, share, modes), jnp.float32),
+            pltpu.VMEM((parts, per_plane, rows, modes), jnp.float32),
+            message, message, message, message,
+            dma((chunks, count)),
+            dma((chunks, count)),
+            dma((chunks,)),
+            dma((chunks,)),
+            dma((chunks,)),
+            dma((chunks,)),
+            dma((chunks,)),
+            dma((chunks, per_plane)),
+            dma((chunks, per_plane)),
+            dma((chunks,)),
+        ],
+        compiler_params=pltpu.CompilerParams(
+            vmem_limit_bytes=44 * 1024 * 1024, collective_id=0, has_side_effects=True
+        ),
+    )(rhs, local, steps, full)
 
 
 def body(wa, gx, field_a, field_b, keep_mask, block_inv, lower_mult):
@@ -238,16 +476,18 @@
         return lax.all_to_all(field, "gx", split_axis=1, concat_axis=1, tiled=True)
 
     rhs = front(spread(field_a), spread(field_b), keep)
+    if wa == 8 and gx == KXT and rows == padded and 2 * rows >= block_inv.shape[1]:
+        solved = solve_across(wa, gx, rhs, block_inv, lower_mult)
+        solved = solved.reshape(2, 2, 1, rows, modes)
+        return (solved[0], solved[1])
     chunks = wa // 4
     width = modes // chunks
-    if chunks != 2:
-        rhs = jnp.moveaxis(rhs, 2, 4).reshape(2, 2, KXT, share, chunks, width)
-        rhs = jnp.moveaxis(rhs, 4, 2)
+    rhs = jnp.moveaxis(rhs.reshape(2, 2, KXT, share, chunks, width), 4, 2)
     rhs = rhs.reshape(wa * gx, share, width)
     rhs = lax.all_to_all(rhs, ("wa", "gx"), split_axis=0, concat_axis=0, tiled=True)
     rhs = rhs.reshape(wa, padded, width)[:, :rows].reshape(wa * rows, width)
     solved = jnp.matmul(
-        solve_matrix(block_inv, lower_mult), rhs, precision=lax.Precision.HIGH
+        solve_matrices(block_inv, lower_mult)[2], rhs, precision=lax.Precision.HIGH
     ).reshape(wa, rows, width)
     solved = lax.all_to_all(solved, "wa", split_axis=0, concat_axis=0, tiled=True)
     solved = solved.reshape(2, 2, chunks, rows, width)

time: 408 us -> 247 us (0.61)
  waiting for transfers between devices: 182 us -> 19.2 us
  Pallas kernels: 18.5 us -> 156 us
  blocking collectives: 137 us -> 0 us
  matrix products: 17.1 us -> 26.7 us
  local copies, waits for them, and re-layouts: 34.9 us -> 27 us
  starting transfers between devices: 17.1 us -> 11.4 us
    pallas_call x0 -> x1, Pallas kernels: none -> 138 us  [solve_across(): pl.pallas_call(functools.partial(solve_kernel, chunks, planes, per_plane,...]
    all_to_all x1 -> x0, blocking collectives: 137 us -> none  [body(): lax.all_to_all(solved, 'wa', split_axis=0, concat_axis=0, tiled=True)]
    all_to_all x1 -> x0, waiting for transfers between devices: 122 us -> none  [body(): lax.all_to_all(rhs, ('wa', 'gx'), split_axis=0, concat_axis=0, tiled=True)]
    all_to_all x2, waiting for transfers between devices: 60.3 us -> 19.2 us  [spread(): return lax.all_to_all(field, 'gx', split_axis=1, concat_axis=1, tiled=True)]
    squeeze x2 -> x0, local copies, waits for them, and re-layouts: 10.3 us -> none  [body(): return (solved[0], solved[1])]
    dot_general x12, matrix products: 17.1 us -> 26.7 us  [the longest x5 8.59 us: solve_matrices(): reduced.append(eye[j] - dot(lower_mult[j - 1], reduced[-1]))]
    slice x3 -> x0, local copies, waits for them, and re-layouts: 8.11 us -> none  [body(): return (solved[0], solved[1])]
    all_to_all x1 -> x0, starting transfers between devices: 7.18 us -> none  [body(): lax.all_to_all(rhs, ('wa', 'gx'), split_axis=0, concat_axis=0, tiled=True)]
  transfers between devices with their start and end apart: 3 -> 2, of which waited for: 3 -> 2; matrix products, arithmetic and copies ran while one was open for 3% -> 19% of each run, Pallas kernels for 0% -> 0%
where the time goes in v3:
time: 247 us; the launch traced here: 245 us
  Pallas kernels  156 us (63%)
  local copies, waits for them, and re-layouts  27 us (11%)
  matrix products  26.7 us (11%)
  waiting for transfers between devices  19.2 us (8%)
  starting transfers between devices  11.4 us (5%)
  other arithmetic  3.83 us (2%)
    pallas_call x1, Pallas kernels, solve_across(): pl.pallas_call(functools.partial(solve_kernel, chunks, planes, per_plane,...  138 us
    all_to_all x2, waiting for transfers between devices, spread(): return lax.all_to_all(field, 'gx', split_axis=1, concat_axis=1, tiled=True)  19.2 us
    pallas_call x1, Pallas kernels, front(): pl.pallas_call(front_kernel, grid=(rows // ROWS,), out_shape=jax.ShapeDty...  18.5 us
    all_to_all x2, starting transfers between devices, spread(): return lax.all_to_all(field, 'gx', split_axis=1, concat_axis=1, tiled=True)  11.4 us
    unnamed x24, local copies, waits for them, and re-layouts  9.45 us
    dot_general x5, matrix products, solve_matrices(): reduced.append(eye[j] - dot(lower_mult[j - 1], reduced[-1]))  8.59 us
    dot_general x1, matrix products, solve_matrices(): dot(back, dot(block_inv, reduced).reshape(count * width, count * width))  7.51 us
    another operation x2, local copies, waits for them, and re-layouts, spread(): field = field.reshape(2, gx, share, modes)  7.39 us
  transfers between devices with their start and end apart: 2, of which 2 were waited for; matrix products, arithmetic and copies ran while one was open for 19% of the time, Pallas kernels for 0%

profile of v3, /device:TPU:4, one launch (start us, length us, event | category | flops | bytes accessed | tf_op | source)
XLA Modules:
  0.0 245.1 jit_solution(1947103304847329033)
XLA Ops:
  0.6 0.0 copy-start
  0.6 3.7 %copy.16 = f32[2,4,24,3840]{3,2,0,1:T(8,128)} copy(f32[2,4,24,3840]{3,2,1,0:T(8,128)} %bitcast.124) | data formatting | bytes 5898240 | tf_op jit(solution)/shard_map/reshape;reshape | solution.py:475
  4.4 4.6 %all-to-all-start = ((f32[2,4,24,3840]{3,2,0,1:T(8,128)}), f32[2,4,24,3840]{3,2,0,1:T(8,128)}, u32[]{:S(2)}, u32[]{:S(2)}) async-start(f32[2,4,24,3840]{3,2,0,1:T(8,128)} %copy.16), calls=%async_computation | async-start | bytes 5898240 | tf_op jit(solution)/shard_map/all_to_all | solution.py:476
  9.0 1.2 iota_compare_fusion
  10.1 1.3 fusion.5
  11.4 1.4 fusion.4
  12.8 3.7 %copy.17 = f32[2,4,24,3840]{3,2,0,1:T(8,128)} copy(f32[2,4,24,3840]{3,2,1,0:T(8,128)} %bitcast.125) | data formatting | bytes 5898240 | tf_op jit(solution)/shard_map/reshape;reshape | solution.py:475
  16.5 0.0 copy-start.7
  16.5 1.4 fusion.3
  17.9 1.4 fusion.2
  19.3 0.0 copy-done.7
  19.3 1.3 fusion.1
  20.6 0.8 constant_dynamic-update-slice_fusion.3
  21.4 0.8 constant_dynamic-update-slice_fusion.2
  22.2 0.8 constant_dynamic-update-slice_fusion.1
  23.0 0.8 constant_dynamic-update-slice_fusion
  23.7 0.8 bitcast_dynamic-update-slice_fusion.4
  24.5 1.9 bitcast_dynamic-update-slice_fusion.3
  26.4 1.3 bitcast_dynamic-update-slice_fusion.2
  27.7 1.2 bitcast_dynamic-update-slice_fusion.1
  28.9 12.4 %all-to-all-done = f32[2,4,24,3840]{3,2,0,1:T(8,128)} async-done(((f32[2,4,24,3840]{3,2,0,1:T(8,128)}), f32[2,4,24,3840]{3,2,0,1:T(8,128)}, u32[]{:S(2)}, u32[]{:S(2)}) %all-to-all-start) | async-done | bytes 2949152 | tf_op jit(solution)/shard_map/all_to_all | solution.py:476
  41.3 6.8 %all-to-all-start.1 = ((f32[2,4,24,3840]{3,2,0,1:T(8,128)}), f32[2,4,24,3840]{3,2,0,1:T(8,128)}, u32[]{:S(2)}, u32[]{:S(2)}) async-start(f32[2,4,24,3840]{3,2,0,1:T(8,128)} %copy.17), calls=%async_computation.1 | async-start | bytes 5898240 | tf_op jit(solution)/shard_map/all_to_all | solution.py:476
  48.1 0.8 slice_dynamic-update-slice_fusion
  48.9 2.1 bitcast_dynamic-update-slice_fusion
  51.0 2.1 fusion.8
  53.2 0.0 copy-done
  53.2 3.9 %fusion.36 = f32[6,768,128]{1,2,0:T(8,128)S(1)} fusion(f32[6,128,768]{2,1,0:T(8,128)} %fusion.8, f32[6,128,128]{2,1,0:T(8,128)S(1)} %copy-done), kind=kOutput, calls=%fused_computation.65 | convolution fusion | flops 905969664 | bytes 5111808 | tf_op jit(solution)/shard_map/dot_general | solution.py:222
  57.1 0.0 copy-start.8
  57.1 7.5 %fusion.37 = f32[768,768]{1,0:T(8,128)S(1)} fusion(f32[768,768]{1,0:T(8,128)} %slice_dynamic-update-slice_fusion, f32[768,768]{1,0:T(8,128)S(1)} %bitcast.123), kind=kOutput, calls=%fused_computation.66 | convolution fusion | flops 5435817984 | bytes 7077888 | tf_op jit(solution)/shard_map/dot_general | solution.py:222
  64.6 0.1 dynamic_slice.25
  64.7 0.7 dynamic_slice.26
  65.4 1.5 dynamic_slice.27
  66.9 0.1 dynamic_slice.22
  67.1 0.0 copy-done.8
  67.1 1.0 dynamic_slice.21
  68.1 0.9 dynamic-slice_bitcast_fusion.1
  69.0 0.8 dynamic-slice_bitcast_fusion
  69.9 1.1 maximum_select_fusion.1
  70.9 0.7 maximum_select_fusion.local_ref
  71.6 0.9 pad_maximum_fusion.full_ref
  72.5 2.0 copy.18.a_ref
  74.6 0.0 copy-start.6
  74.6 6.8 %all-to-all-done.1 = f32[2,4,24,3840]{3,2,0,1:T(8,128)} async-done(((f32[2,4,24,3840]{3,2,0,1:T(8,128)}), f32[2,4,24,3840]{3,2,0,1:T(8,128)}, u32[]{:S(2)}, u32[]{:S(2)}) %all-to-all-start.1) | async-done | bytes 2949152 | tf_op jit(solution)/shard_map/all_to_all | solution.py:476
  81.4 0.0 copy-start.4
  81.4 0.0 copy-start.5
  81.4 2.1 copy.19.b_ref
  83.5 0.0 copy-done.6
  83.5 0.0 copy-done.4
  83.5 0.0 copy-done.5
  83.5 0.0 copy-start.2
  83.5 0.0 copy-start.3
  83.6 18.5 %shard_map.95.rhs_ref = f32[2,2,4,24,3840]{4,3,2,1,0:T(8,128)S(1)} custom-call(f32[2,4,24,3840]{3,2,1,0:T(8,128)S(1)} %copy.18.a_ref, f32[2,4,24,3840]{3,2,1,0:T(8,128)S(1)} %copy.19.b_ref, f32[1,3840]{1,0:T(1,128)S(1)} %reshape.35.keep_ref, f32[2,45,128]{2,1,0:T(8,128)S(1)} %copy-done.6, bf16[2,256,256]{2,1,0:T(8,128)(2,1)S(1)} %copy-done.4, ...), custom_call_target="tpu_custom_call" | custom-call | flops 6794772480 | bytes 6291456 | tf_op jit(solution)/shard_map/pallas_call | solution.py:183
  102.1 0.0 copy-start.1
  102.1 2.5 %copy-done.1 = f32[2,2,4,24,3840]{4,3,2,1,0:T(8,128)} copy-done((f32[2,2,4,24,3840]{4,3,2,1,0:T(8,128)}, f32[2,2,4,24,3840]{4,3,2,1,0:T(8,128)S(1)}, u32[]{:S(2)}) %copy-start.1) | copy-done | bytes 5898264
  104.6 0.0 copy-done.2
  104.6 0.0 copy-done.3
  104.6 137.5 %shard_map.96 = f32[4,96,3840]{2,1,0:T(8,128)S(1)} custom-call(f32[2,2,4,24,3840]{4,3,2,1,0:T(8,128)} %copy-done.1, f32[256,192]{1,0:T(8,128)S(1)} %copy-done.3, f32[2,128,128]{2,1,0:T(8,128)S(1)} %maximum_select_fusion.2.step_ref, f32[192,448]{1,0:T(8,128)S(1)} %copy-done.2), custom_call_target="tpu_custom_call" | custom-call | tf_op jit(solution)/shard_map/pallas_call | solution.py:439
  242.2 3.0 %slice_bitcast_fusion = (f32[2,1,96,3840]{3,2,1,0:T(8,128)}, f32[2,1,96,3840]{3,2,1,0:T(8,128)}) fusion(f32[4,96,3840]{2,1,0:T(8,128)S(1)} %shard_map.96), kind=kLoop, calls=%fused_computation | loop fusion | bytes 11796480
  (3 shorter events, 0.0 us)
Async XLA Ops:
  0.6 52.5 %copy-start = (f32[6,128,128]{2,1,0:T(8,128)S(1)}, f32[6,128,128]{2,1,0:T(8,128)}, u32[]{:S(2)}) copy-start(f32[6,128,128]{2,1,0:T(8,128)} %param.11) | copy-start | bytes 1179652
  4.4 36.9 %all-to-all-start = ((f32[2,4,24,3840]{3,2,0,1:T(8,128)}), f32[2,4,24,3840]{3,2,0,1:T(8,128)}, u32[]{:S(2)}, u32[]{:S(2)}) async-start(f32[2,4,24,3840]{3,2,0,1:T(8,128)} %copy.16), calls=%async_computation | async-start | bytes 5898240 | tf_op jit(solution)/shard_map/all_to_all | solution.py:476
  16.5 2.8 %copy-start.7 = (f32[5,128,128]{2,1,0:T(8,128)S(1)}, f32[5,128,128]{2,1,0:T(8,128)}, u32[]{:S(2)}) copy-start(f32[5,128,128]{2,1,0:T(8,128)} %param.12) | copy-start | bytes 983044
  41.3 40.1 %all-to-all-start.1 = ((f32[2,4,24,3840]{3,2,0,1:T(8,128)}), f32[2,4,24,3840]{3,2,0,1:T(8,128)}, u32[]{:S(2)}, u32[]{:S(2)}) async-start(f32[2,4,24,3840]{3,2,0,1:T(8,128)} %copy.17), calls=%async_computation.1 | async-start | bytes 5898240 | tf_op jit(solution)/shard_map/all_to_all | solution.py:476
  57.1 10.0 %copy-start.8 = (s32[3840]{0:T(1024)S(1)}, s32[3840]{0:T(1024)}, u32[]{:S(2)}) copy-start(s32[3840]{0:T(1024)} %param.10) | copy-start | bytes 46084
  74.6 8.9 %copy-start.6 = (f32[2,45,128]{2,1,0:T(8,128)S(1)}, f32[2,45,128]{2,1,0:T(8,128)}, u32[]{:S(2)}) copy-start(f32[2,45,128]{2,1,0:T(8,128)} %constant.72.clone.twist_ref) | copy-start | bytes 138244
  81.4 2.1 copy-start.4
  81.4 2.1 copy-start.5
  83.5 21.1 %copy-start.2 = (f32[192,448]{1,0:T(8,128)S(1)}, f32[192,448]{1,0:T(8,128)}, u32[]{:S(2)}) copy-start(f32[192,448]{1,0:T(8,128)} %pad_maximum_fusion.full_ref) | copy-start | bytes 1032196
  83.5 21.1 %copy-start.3 = (f32[256,192]{1,0:T(8,128)S(1)}, f32[256,192]{1,0:T(8,128)}, u32[]{:S(2)}) copy-start(f32[256,192]{1,0:T(8,128)} %maximum_select_fusion.local_ref) | copy-start | bytes 589828
  102.1 2.5 %copy-start.1 = (f32[2,2,4,24,3840]{4,3,2,1,0:T(8,128)}, f32[2,2,4,24,3840]{4,3,2,1,0:T(8,128)S(1)}, u32[]{:S(2)}) copy-start(f32[2,2,4,24,3840]{4,3,2,1,0:T(8,128)S(1)} %shard_map.95.rhs_ref) | copy-start | bytes 17694724

commit v4 on v3

--- a/solution.py
+++ b/solution.py
@@ -96,14 +96,14 @@
     return dot(hi, w_hi) + (dot(lo, w_hi) + dot(hi, w_lo))
 
 
-def front_kernel(a_ref, b_ref, keep_ref, twist_ref, winv_ref, wfwd_ref, out_ref,
+def front_kernel(slab_ref, keep_ref, twist_ref, winv_ref, wfwd_ref, earlier_ref, out_ref,
                  plane_ref, mid_ref, za_ref, zb_ref, hat_ref):
     half = 15
     tile = (ROWS, LANES)
-    for f, ref in enumerate((a_ref, b_ref)):
+    for f in range(2):
         for t in range(30):
             cols = pl.ds(t * LANES, LANES)
-            ins = [(ref[0, k, :, cols], ref[1, k, :, cols]) for k in range(KXT)]
+            ins = [(slab_ref[k, f, 0, :, cols], slab_ref[k, f, 1, :, cols]) for k in range(KXT)]
             for x, value in enumerate(dft4(ins, 1)):
                 plane_ref[x, f, t, 0], plane_ref[x, f, t, 1] = value
 
@@ -146,14 +146,16 @@
         return carry
 
     lax.fori_loop(0, KXT, one_plane, 0)
-    for f, ref in enumerate((a_ref, b_ref)):
+    for f in range(2):
         for t in range(30):
             cols = pl.ds(t * LANES, LANES)
             keep = keep_ref[:, cols]
             ins = [(hat_ref[x, f, t, 0], hat_ref[x, f, t, 1]) for x in range(KXT)]
             for k, value in enumerate(dft4(ins, -1)):
                 for part in range(2):
-                    out_ref[f, part, k, :, cols] = ref[part, k, :, cols] + value[part] * keep
+                    out_ref[f, part, k, :, cols] = (
+                        slab_ref[k, f, part, :, cols] + value[part] * keep
+                    )
 
 
 def front_tables(modes):
@@ -174,25 +176,34 @@
     return np.stack([np.cos(twist), np.sin(twist)]).astype(np.float32), halves(inv), halves(fwd)
 
 
-def front(slab_a, slab_b, keep):
-    _, kxt, rows, modes = slab_a.shape
+def front(slab, keep, all_rows, first_row, earlier):
+    kxt, _, _, rows, modes = slab.shape
+    first = first_row // ROWS
     assert kxt == KXT and modes == 30 * LANES and rows % ROWS == 0
     twist, inv, fwd = front_tables(modes)
     points = 45
-    field_spec = pl.BlockSpec((2, KXT, ROWS, modes), lambda i: (0, 0, i, 0))
+    block = (2, 2, KXT, ROWS, modes)
+    slab_block = (KXT, 2, 2, ROWS, modes)
+    result = jax.ShapeDtypeStruct((2, 2, KXT, all_rows, modes), jnp.float32)
+    if earlier is None:
+        earlier = jnp.zeros((ROWS, LANES), jnp.float32)
+        aliases = {}
+    else:
+        aliases = {5: 0}
     return pl.pallas_call(
         front_kernel,
         grid=(rows // ROWS,),
-        out_shape=jax.ShapeDtypeStruct((2, 2, KXT, rows, modes), jnp.float32),
+        out_shape=result,
+        input_output_aliases=aliases,
         in_specs=[
-            field_spec,
-            field_spec,
+            pl.BlockSpec(slab_block, lambda i: (0, 0, 0, i, 0)),
             pl.BlockSpec((1, modes), lambda i: (0, 0)),
             pl.BlockSpec(twist.shape, lambda i: (0, 0, 0)),
             pl.BlockSpec(inv.shape, lambda i: (0, 0, 0)),
             pl.BlockSpec(fwd.shape, lambda i: (0, 0, 0)),
+            pl.BlockSpec(memory_space=pl.ANY),
         ],
-        out_specs=pl.BlockSpec((2, 2, KXT, ROWS, modes), lambda i: (0, 0, 0, i, 0)),
+        out_specs=pl.BlockSpec(block, lambda i: (0, 0, 0, i + first, 0)),
         scratch_shapes=[
             pltpu.VMEM((KXT, 2, 30, 2, ROWS, LANES), jnp.float32),
             pltpu.VMEM((5, 9, 2, ROWS, LANES), jnp.float32),
@@ -204,7 +215,7 @@
         cost_estimate=pl.CostEstimate(
             flops=rows * 32 * 5760 * 256 * 6, bytes_accessed=rows * 2**18, transcendentals=0
         ),
-    )(slab_a, slab_b, keep, jnp.asarray(twist), jnp.asarray(inv), jnp.asarray(fwd))
+    )(slab, keep, jnp.asarray(twist), jnp.asarray(inv), jnp.asarray(fwd), earlier)
 
 
 def solve_matrices(block_inv, lower_mult):
@@ -430,7 +441,7 @@
     steps = ordered(up_step[None], down_step[None], 0)
     full = jnp.concatenate([cut(dense, first, plane, first, plane),
                             ordered(up_full, down_full, 1)], axis=1)
-    lanes = 6 * LANES
+    lanes = 3 * LANES
     chunks = parts * modes // lanes
     dma = pltpu.SemaphoreType.DMA
     vmem = pl.BlockSpec(memory_space=pltpu.VMEM)
@@ -472,10 +483,21 @@
         field = field.reshape(2, rows, modes)
         if padded != rows:
             field = jnp.pad(field, ((0, 0), (0, padded - rows), (0, 0)))
-        field = field.reshape(2, gx, share, modes)
-        return lax.all_to_all(field, "gx", split_axis=1, concat_axis=1, tiled=True)
-
-    rhs = front(spread(field_a), spread(field_b), keep)
+        return field.reshape(2, gx, share, modes)
+
+    fields = (spread(field_a), spread(field_b))
+    cut = share // ROWS * 2 // 3 * ROWS
+    rhs, slab = None, None
+    for first, last in ((0, cut), (cut, share)):
+        if first < last:
+            part = jnp.stack([field[:, :, first:last] for field in fields])
+            part = jnp.moveaxis(part, 2, 0)
+            if slab is not None:
+                part, slab = lax.optimization_barrier((part, slab))
+                rhs = front(slab, keep, share, 0, None)
+            slab = lax.all_to_all(part, "gx", split_axis=0, concat_axis=0, tiled=True)
+            begin = first
+    rhs = front(slab, keep, share, begin, rhs)
     if wa == 8 and gx == KXT and rows == padded and 2 * rows >= block_inv.shape[1]:
         solved = solve_across(wa, gx, rhs, block_inv, lower_mult)
         solved = solved.reshape(2, 2, 1, rows, modes)

time: 247 us -> 246 us (level)
  matrix products: 26.7 us -> 23 us
  local copies, waits for them, and re-layouts: 27 us -> 29.8 us
    unnamed x24 -> x30, local copies, waits for them, and re-layouts: 9.45 us -> 17.9 us
    all_to_all x2 -> x0, local copies, waits for them, and re-layouts: 4.12 us -> none  [spread(): return lax.all_to_all(field, 'gx', split_axis=1, concat_axis=1, tiled=True)]
    dot_general x5, matrix products: 6.75 us -> 3.21 us  [solve_matrices(): back.insert(0, eye[j] - dot(lower_mult[j].T, back[0]))]
    transpose x0 -> x2, other arithmetic: none -> 3.53 us  [body(): part = jnp.moveaxis(part, 2, 0)]
    another operation x2, local copies, waits for them, and re-layouts: 7.39 us -> 4.1 us  [body(): part = jnp.stack([field[:, :, first:last] for field in fields])]
    dot_general x5, matrix products: 8.59 us -> 6.05 us  [solve_matrices(): reduced.append(eye[j] - dot(lower_mult[j - 1], reduced[-1]))]
    pallas_call x1 -> x2, Pallas kernels: 18.5 us -> 19.7 us  [front(): pl.pallas_call(front_kernel, grid=(rows // ROWS,), out_shape=result, inpu...]
  transfers between devices with their start and end apart: 2 -> 2, of which waited for: 2 -> 1; matrix products, arithmetic and copies ran while one was open for 19% -> 16% of each run, Pallas kernels for 0% -> 6%
where the time goes in v4:
time: 246 us; the launch traced here: 243 us
  Pallas kernels  156 us (63%)
  local copies, waits for them, and re-layouts  29.8 us (12%)
  matrix products  23 us (9%)
  waiting for transfers between devices  18.6 us (8%)
  starting transfers between devices  10.7 us (4%)
  other arithmetic  4.98 us (2%)
    pallas_call x1, Pallas kernels, solve_across(): pl.pallas_call(functools.partial(solve_kernel, chunks, planes, per_plane,...  136 us
    pallas_call x2, Pallas kernels, front(): pl.pallas_call(front_kernel, grid=(rows // ROWS,), out_shape=result, inpu...  19.7 us
    all_to_all x2, waiting for transfers between devices, body(): slab = lax.all_to_all(part, 'gx', split_axis=0, concat_axis=0, tiled=True)  18.6 us
    unnamed x30, local copies, waits for them, and re-layouts  17.9 us
    all_to_all x2, starting transfers between devices, body(): slab = lax.all_to_all(part, 'gx', split_axis=0, concat_axis=0, tiled=True)  10.7 us
    dot_general x1, matrix products, solve_matrices(): dot(back, dot(block_inv, reduced).reshape(count * width, count * width))  8.4 us
    dot_general x5, matrix products, solve_matrices(): reduced.append(eye[j] - dot(lower_mult[j - 1], reduced[-1]))  6.05 us
    dot_general x1, matrix products, solve_matrices(): dot(block_inv, reduced).reshape(count * width, count * width)  5.32 us
  transfers between devices with their start and end apart: 2, of which 1 were waited for; matrix products, arithmetic and copies ran while one was open for 16% of the time, Pallas kernels for 6%

profile of v4, /device:TPU:4, one launch (start us, length us, event | category | flops | bytes accessed | tf_op | source)
XLA Modules:
  0.0 243.4 jit_solution(9159526231818821144)
XLA Ops:
  0.6 0.0 copy-start
  0.6 2.4 %copy_bitcast_fusion = (f32[1,2,4,16,3840]{4,3,1,0,2:T(8,128)S(1)}, f32[1,2,4,16,3840]{4,3,1,0,2:T(8,128)S(1)}) fusion(f32[2,4,24,3840]{3,2,1,0:T(8,128)} %bitcast.136, f32[2,4,24,3840]{3,2,1,0:T(8,128)} %bitcast.138), kind=kLoop, calls=%fused_computation.5 | loop fusion | bytes 7864320 | tf_op jit(solution)/shard_map/stack | solution.py:493
  3.1 2.1 maximum_bitcast_fusion
  5.2 4.8 %all-to-all-start = ((f32[4,2,2,16,3840]{4,3,2,1,0:T(8,128)}), f32[4,2,2,16,3840]{4,3,2,1,0:T(8,128)}, u32[]{:S(2)}, u32[]{:S(2)}) async-start(f32[4,2,2,16,3840]{4,3,2,1,0:T(8,128)} %maximum_bitcast_fusion), calls=%async_computation | async-start | bytes 7864320 | tf_op jit(solution)/shard_map/all_to_all | solution.py:498
  10.0 0.0 copy-start.9
  10.0 0.3 iota_compare_fusion
  10.4 0.8 bitcast_dynamic-update-slice_fusion.4
  11.1 0.0 copy-done.9
  11.1 0.4 fusion.5
  11.5 0.5 fusion.4
  12.1 0.5 fusion.3
  12.6 0.5 fusion.2
  13.1 1.3 fusion.1
  14.4 0.8 constant_dynamic-update-slice_fusion.3
  15.2 0.0 copy-start.11
  15.2 0.8 constant_dynamic-update-slice_fusion.2
  15.9 0.8 constant_dynamic-update-slice_fusion.1
  16.7 0.8 constant_dynamic-update-slice_fusion
  17.5 1.1 bitcast_dynamic-update-slice_fusion.3
  18.6 0.8 slice_dynamic-update-slice_fusion
  19.3 0.0 copy-done.11
  19.4 1.5 dynamic_slice.27
  20.9 1.2 bitcast_dynamic-update-slice_fusion.2
  22.2 1.2 bitcast_dynamic-update-slice_fusion.1
  23.4 1.2 bitcast_dynamic-update-slice_fusion
  24.6 1.2 fusion.8
  25.9 0.0 copy-done
  25.9 5.3 %fusion.36 = f32[6,768,128]{1,2,0:T(8,128)} fusion(f32[6,128,768]{2,1,0:T(8,128)} %fusion.8, f32[6,128,128]{2,1,0:T(8,128)S(1)} %copy-done), kind=kOutput, calls=%fused_computation.71 | convolution fusion | flops 905969664 | bytes 5111808 | tf_op jit(solution)/shard_map/dot_general | solution.py:233
  31.2 1.6 copy_bitcast_fusion.2
  32.9 1.4 maximum_bitcast_fusion.1
  34.2 18.6 %all-to-all-done.slab_ref = f32[4,2,2,16,3840]{4,3,2,1,0:T(8,128)} async-done(((f32[4,2,2,16,3840]{4,3,2,1,0:T(8,128)}), f32[4,2,2,16,3840]{4,3,2,1,0:T(8,128)}, u32[]{:S(2)}, u32[]{:S(2)}) %all-to-all-start) | async-done | bytes 3932192 | tf_op jit(solution)/shard_map/all_to_all | solution.py:498
  52.9 5.9 %all-to-all-start.1 = ((f32[4,2,2,8,3840]{4,3,2,1,0:T(8,128)}), f32[4,2,2,8,3840]{4,3,2,1,0:T(8,128)S(1)}, u32[]{:S(2)}, u32[]{:S(2)}) async-start(f32[4,2,2,8,3840]{4,3,2,1,0:T(8,128)} %maximum_bitcast_fusion.1), calls=%async_computation.1 | async-start | bytes 3932160 | tf_op jit(solution)/shard_map/all_to_all | solution.py:498
  58.7 0.0 copy-start.10
  58.7 8.4 %fusion.37 = f32[768,768]{1,0:T(8,128)S(1)} fusion(f32[768,768]{1,0:T(8,128)} %slice_dynamic-update-slice_fusion, f32[768,768]{1,0:T(8,128)} %bitcast.135), kind=kOutput, calls=%fused_computation.72 | convolution fusion | flops 5435817984 | bytes 7077888 | tf_op jit(solution)/shard_map/dot_general | solution.py:233
  67.1 0.0 copy-start.8
  67.2 1.4 copy-done.8
  68.6 0.0 copy-start.4
  68.6 0.0 copy-start.7
  68.6 0.8 dynamic_slice.25
  69.4 0.9 dynamic_slice.26
  70.3 1.0 dynamic_slice.22
  71.3 1.0 dynamic_slice.21
  72.3 0.9 dynamic-slice_bitcast_fusion
  73.2 0.8 dynamic-slice_bitcast_fusion.1
  74.1 0.0 copy-done.10
  74.1 1.1 pad_maximum_fusion.full_ref
  75.2 0.0 copy-done.4
  75.2 0.0 copy-done.7
  75.2 0.0 copy-start.5
  75.2 0.9 copy-done.5
  76.2 13.6 %shard_map.122.earlier_ref = f32[2,2,4,24,3840]{4,3,2,1,0:T(8,128)S(1)} custom-call(f32[4,2,2,16,3840]{4,3,2,1,0:T(8,128)} %all-to-all-done.slab_ref, f32[1,3840]{1,0:T(1,128)S(1)} %reshape.35.keep_ref, f32[2,45,128]{2,1,0:T(8,128)S(1)} %copy-done.7, bf16[2,256,256]{2,1,0:T(8,128)(2,1)S(1)} %copy-done.5, bf16[2,256,256]{2,1,0:T(8,128)(2,1)S(1)} %copy-done.4, ...), custom_call_target="tpu_custom_call" | custom-call | flops 4529848320 | bytes 4194304 | tf_op jit(solution)/shard_map/pallas_call | solution.py:193
  89.8 0.0 copy-start.1
  89.8 2.5 %copy-done.1 = f32[2,2,4,24,3840]{4,3,2,1,0:T(8,128)} copy-done((f32[2,2,4,24,3840]{4,3,2,1,0:T(8,128)}, f32[2,2,4,24,3840]{4,3,2,1,0:T(8,128)S(1)}, u32[]{:S(2)}) %copy-start.1) | copy-done | bytes 5898264
  92.3 0.0 all-to-all-done.1.slab_ref
  92.3 0.0 copy-start.2
  92.3 2.7 %copy-done.2 = f32[2,2,4,24,3840]{4,3,2,1,0:T(8,128)S(1)} copy-done((f32[2,2,4,24,3840]{4,3,2,1,0:T(8,128)S(1)}, f32[2,2,4,24,3840]{4,3,2,1,0:T(8,128)}, u32[]{:S(2)}) %copy-start.2) | copy-done | bytes 5898264
  95.0 0.0 copy-start.6
  95.0 0.9 copy-done.6
  96.0 6.0 %shard_map.123.rhs_ref = f32[2,2,4,24,3840]{4,3,2,1,0:T(8,128)S(1)} custom-call(f32[4,2,2,8,3840]{4,3,2,1,0:T(8,128)S(1)} %all-to-all-done.1.slab_ref, f32[1,3840]{1,0:T(1,128)S(1)} %reshape.35.keep_ref, f32[2,45,128]{2,1,0:T(8,128)S(1)} %copy-done.7, bf16[2,256,256]{2,1,0:T(8,128)(2,1)S(1)} %copy-done.6, ...), custom_call_target="tpu_custom_call", output_to_operand_aliasing={{}: (5, {})} | custom-call | flops 2264924160 | bytes 2097152 | tf_op jit(solution)/shard_map/pallas_call | solution.py:193
  102.0 0.0 copy-start.3
  102.0 2.5 %copy-done.3 = f32[2,2,4,24,3840]{4,3,2,1,0:T(8,128)} copy-done((f32[2,2,4,24,3840]{4,3,2,1,0:T(8,128)}, f32[2,2,4,24,3840]{4,3,2,1,0:T(8,128)S(1)}, u32[]{:S(2)}) %copy-start.3) | copy-done | bytes 5898264
  104.6 135.9 %shard_map.124 = f32[4,96,3840]{2,1,0:T(8,128)S(1)} custom-call(f32[2,2,4,24,3840]{4,3,2,1,0:T(8,128)} %copy-done.3, f32[256,192]{1,0:T(8,128)S(1)} %maximum_select_fusion.local_ref, f32[2,128,128]{2,1,0:T(8,128)S(1)} %maximum_select_fusion.2.step_ref, f32[192,448]{1,0:T(8,128)S(1)} %pad_maximum_fusion.full_ref), custom_call_target="tpu_custom_call" | custom-call | tf_op jit(solution)/shard_map/pallas_call | solution.py:450
  240.4 3.0 %slice_bitcast_fusion = (f32[2,1,96,3840]{3,2,1,0:T(8,128)}, f32[2,1,96,3840]{3,2,1,0:T(8,128)}) fusion(f32[4,96,3840]{2,1,0:T(8,128)S(1)} %shard_map.124), kind=kLoop, calls=%fused_computation.1 | loop fusion | bytes 11796480
  (6 shorter events, 0.1 us)
Async XLA Ops:
  0.6 25.3 %copy-start = (f32[6,128,128]{2,1,0:T(8,128)S(1)}, f32[6,128,128]{2,1,0:T(8,128)}, u32[]{:S(2)}) copy-start(f32[6,128,128]{2,1,0:T(8,128)} %param.14) | copy-start | bytes 1179652
  5.2 47.6 %all-to-all-start = ((f32[4,2,2,16,3840]{4,3,2,1,0:T(8,128)}), f32[4,2,2,16,3840]{4,3,2,1,0:T(8,128)}, u32[]{:S(2)}, u32[]{:S(2)}) async-start(f32[4,2,2,16,3840]{4,3,2,1,0:T(8,128)} %maximum_bitcast_fusion), calls=%async_computation | async-start | bytes 7864320 | tf_op jit(solution)/shard_map/all_to_all | solution.py:498
  10.0 1.1 copy-start.9
  15.2 4.2 %copy-start.11 = (s32[3840]{0:T(1024)S(1)}, s32[3840]{0:T(1024)}, u32[]{:S(2)}) copy-start(s32[3840]{0:T(1024)} %param.13) | copy-start | bytes 46084
  52.9 39.5 %all-to-all-start.1 = ((f32[4,2,2,8,3840]{4,3,2,1,0:T(8,128)}), f32[4,2,2,8,3840]{4,3,2,1,0:T(8,128)S(1)}, u32[]{:S(2)}, u32[]{:S(2)}) async-start(f32[4,2,2,8,3840]{4,3,2,1,0:T(8,128)} %maximum_bitcast_fusion.1), calls=%async_computation.1 | async-start | bytes 3932160 | tf_op jit(solution)/shard_map/all_to_all | solution.py:498
  58.7 15.3 %copy-start.10 = (f32[192,128]{1,0:T(8,128)S(1)}, f32[192,128]{1,0:T(8,128)}, u32[]{:S(2)}) copy-start(f32[192,128]{1,0:T(8,128)} %dynamic_slice.27) | copy-start | bytes 294916
  67.1 1.4 copy-start.8
  68.6 6.6 %copy-start.4 = (bf16[2,256,256]{2,1,0:T(8,128)(2,1)S(1)}, bf16[2,256,256]{2,1,0:T(8,128)(2,1)}, u32[]{:S(2)}) copy-start(bf16[2,256,256]{2,1,0:T(8,128)(2,1)} %constant.76.clone.wfwd_ref) | copy-start | bytes 786436
  68.6 6.6 %copy-start.7 = (f32[2,45,128]{2,1,0:T(8,128)S(1)}, f32[2,45,128]{2,1,0:T(8,128)}, u32[]{:S(2)}) copy-start(f32[2,45,128]{2,1,0:T(8,128)} %constant.74.clone.twist_ref) | copy-start | bytes 138244
  75.2 1.0 copy-start.5
  89.8 2.5 %copy-start.1 = (f32[2,2,4,24,3840]{4,3,2,1,0:T(8,128)}, f32[2,2,4,24,3840]{4,3,2,1,0:T(8,128)S(1)}, u32[]{:S(2)}) copy-start(f32[2,2,4,24,3840]{4,3,2,1,0:T(8,128)S(1)} %shard_map.122.earlier_ref) | copy-start | bytes 17694724
  92.3 2.7 %copy-start.2 = (f32[2,2,4,24,3840]{4,3,2,1,0:T(8,128)S(1)}, f32[2,2,4,24,3840]{4,3,2,1,0:T(8,128)}, u32[]{:S(2)}) copy-start(f32[2,2,4,24,3840]{4,3,2,1,0:T(8,128)} %copy-done.1) | copy-start | bytes 17694724
  95.0 0.9 copy-start.6
  102.0 2.5 %copy-start.3 = (f32[2,2,4,24,3840]{4,3,2,1,0:T(8,128)}, f32[2,2,4,24,3840]{4,3,2,1,0:T(8,128)S(1)}, u32[]{:S(2)}) copy-start(f32[2,2,4,24,3840]{4,3,2,1,0:T(8,128)S(1)} %shard_map.123.rhs_ref) | copy-start | bytes 17694724

commit v5 on v4

--- a/solution.py
+++ b/solution.py
@@ -408,12 +408,9 @@
     return dot(l_hi, r_hi) + (dot(l_lo, r_hi) + dot(l_hi, r_lo))
 
 
-def solve_across(wa, gx, rhs, block_inv, lower_mult):
-    share, modes = rhs.shape[-2:]
-    planes, per_plane, parts = 4, 2, 2
-    rows = share * gx
+def plane_matrices(rows, block_inv, lower_mult):
+    planes, per_plane = 4, 2
     plane = per_plane * rows
-    count = per_plane * gx
     nblocks, width = block_inv.shape[:2]
     reduce_op, back_op, dense = solve_matrices(block_inv, lower_mult)
     z = lax.axis_index("wa") // per_plane
@@ -441,6 +438,15 @@
     steps = ordered(up_step[None], down_step[None], 0)
     full = jnp.concatenate([cut(dense, first, plane, first, plane),
                             ordered(up_full, down_full, 1)], axis=1)
+    return local, steps, full
+
+
+def solve_across(wa, gx, rhs, local, steps, full):
+    share, modes = rhs.shape[-2:]
+    planes, per_plane, parts = 4, 2, 2
+    rows = share * gx
+    count = per_plane * gx
+    width = steps.shape[1]
     lanes = 3 * LANES
     chunks = parts * modes // lanes
     dma = pltpu.SemaphoreType.DMA
@@ -487,19 +493,21 @@
 
     fields = (spread(field_a), spread(field_b))
     cut = share // ROWS * 2 // 3 * ROWS
+    chained = wa == 8 and gx == KXT and rows == padded and 2 * rows >= block_inv.shape[1]
+    matrices = plane_matrices(rows, block_inv, lower_mult) if chained else ()
     rhs, slab = None, None
     for first, last in ((0, cut), (cut, share)):
         if first < last:
             part = jnp.stack([field[:, :, first:last] for field in fields])
             part = jnp.moveaxis(part, 2, 0)
             if slab is not None:
-                part, slab = lax.optimization_barrier((part, slab))
+                part, slab, matrices = lax.optimization_barrier((part, slab, matrices))
                 rhs = front(slab, keep, share, 0, None)
             slab = lax.all_to_all(part, "gx", split_axis=0, concat_axis=0, tiled=True)
             begin = first
     rhs = front(slab, keep, share, begin, rhs)
-    if wa == 8 and gx == KXT and rows == padded and 2 * rows >= block_inv.shape[1]:
-        solved = solve_across(wa, gx, rhs, block_inv, lower_mult)
+    if chained:
+        solved = solve_across(wa, gx, rhs, *matrices)
         solved = solved.reshape(2, 2, 1, rows, modes)
         return (solved[0], solved[1])
     chunks = wa // 4

time: 246 us -> 236 us (0.959)
  waiting for transfers between devices: 18.6 us -> 12.6 us
  local copies, waits for them, and re-layouts: 29.8 us -> 25.2 us
    all_to_all x2, waiting for transfers between devices: 18.6 us -> 12.6 us  [body(): slab = lax.all_to_all(part, 'gx', split_axis=0, concat_axis=0, tiled=True)]
    dynamic_slice x5, local copies, waits for them, and re-layouts: 5.29 us -> 2.18 us  [cut(): return lax.dynamic_slice(table, (row, column), (height, span))]
    unnamed x30 -> x26, local copies, waits for them, and re-layouts: 17.9 us -> 16.5 us
  transfers between devices with their start and end apart: 2 -> 2, of which waited for: 1 -> 2; matrix products, arithmetic and copies ran while one was open for 16% -> 15% of each run, Pallas kernels for 6% -> 6%
where the time goes in v5:
time: 236 us; the launch traced here: 233 us
  Pallas kernels  156 us (66%)
  local copies, waits for them, and re-layouts  25.2 us (11%)
  matrix products  22.4 us (9%)
  waiting for transfers between devices  12.6 us (5%)
  starting transfers between devices  10.6 us (4%)
  other arithmetic  4.95 us (2%)
    pallas_call x1, Pallas kernels, solve_across(): pl.pallas_call(functools.partial(solve_kernel, chunks, planes, per_plane,...  136 us
    pallas_call x2, Pallas kernels, front(): pl.pallas_call(front_kernel, grid=(rows // ROWS,), out_shape=result, inpu...  19.7 us
    unnamed x26, local copies, waits for them, and re-layouts  16.5 us
    all_to_all x2, waiting for transfers between devices, body(): slab = lax.all_to_all(part, 'gx', split_axis=0, concat_axis=0, tiled=True)  12.6 us
    all_to_all x2, starting transfers between devices, body(): slab = lax.all_to_all(part, 'gx', split_axis=0, concat_axis=0, tiled=True)  10.6 us
    dot_general x1, matrix products, solve_matrices(): dot(back, dot(block_inv, reduced).reshape(count * width, count * width))  7.7 us
    dot_general x5, matrix products, solve_matrices(): reduced.append(eye[j] - dot(lower_mult[j - 1], reduced[-1]))  6.82 us
  transfers between devices with their start and end apart: 2, of which 2 were waited for; matrix products, arithmetic and copies ran while one was open for 15% of the time, Pallas kernels for 6%

profile of v5, /device:TPU:4, one launch (start us, length us, event | category | flops | bytes accessed | tf_op | source)
XLA Modules:
  0.0 232.8 jit_solution(8171623900961746876)
XLA Ops:
  0.6 0.0 copy-start
  0.6 2.5 %copy_bitcast_fusion = (f32[1,2,4,16,3840]{4,3,1,0,2:T(8,128)S(1)}, f32[1,2,4,16,3840]{4,3,1,0,2:T(8,128)S(1)}) fusion(f32[2,4,24,3840]{3,2,1,0:T(8,128)} %bitcast.136, f32[2,4,24,3840]{3,2,1,0:T(8,128)} %bitcast.138), kind=kLoop, calls=%fused_computation.5 | loop fusion | bytes 7864320 | tf_op jit(solution)/shard_map/stack | solution.py:501
  3.1 2.2 maximum_bitcast_fusion
  5.3 4.8 %all-to-all-start = ((f32[4,2,2,16,3840]{4,3,2,1,0:T(8,128)}), f32[4,2,2,16,3840]{4,3,2,1,0:T(8,128)}, u32[]{:S(2)}, u32[]{:S(2)}) async-start(f32[4,2,2,16,3840]{4,3,2,1,0:T(8,128)} %maximum_bitcast_fusion), calls=%async_computation | async-start | bytes 7864320 | tf_op jit(solution)/shard_map/all_to_all | solution.py:506
  10.1 0.0 copy-start.8
  10.2 1.2 iota_compare_fusion
  11.4 0.8 bitcast_dynamic-update-slice_fusion.4
  12.2 0.0 copy-done.8
  12.2 1.2 fusion.5
  13.3 0.5 fusion.4
  13.9 0.5 fusion.3
  14.4 0.5 fusion.2
  14.9 1.3 fusion.1
  16.2 0.8 constant_dynamic-update-slice_fusion.3
  17.0 0.8 constant_dynamic-update-slice_fusion.2
  17.8 0.8 constant_dynamic-update-slice_fusion.1
  18.5 0.8 constant_dynamic-update-slice_fusion
  19.3 0.8 slice_dynamic-update-slice_fusion
  20.1 1.9 bitcast_dynamic-update-slice_fusion.3
  21.9 1.2 bitcast_dynamic-update-slice_fusion.2
  23.2 1.2 bitcast_dynamic-update-slice_fusion.1
  24.4 1.2 bitcast_dynamic-update-slice_fusion
  25.6 1.2 fusion.8
  26.9 0.9 dynamic_slice.27
  27.8 0.0 copy-done
  27.8 3.9 %fusion.36 = f32[6,768,128]{1,2,0:T(8,128)S(1)} fusion(f32[6,128,768]{2,1,0:T(8,128)} %fusion.8, f32[6,128,128]{2,1,0:T(8,128)S(1)} %copy-done), kind=kOutput, calls=%fused_computation.71 | convolution fusion | flops 905969664 | bytes 5111808 | tf_op jit(solution)/shard_map/dot_general | solution.py:233
  31.7 7.7 %fusion.37 = f32[768,768]{1,0:T(8,128)S(1)} fusion(f32[768,768]{1,0:T(8,128)} %slice_dynamic-update-slice_fusion, f32[768,768]{1,0:T(8,128)S(1)} %bitcast.135), kind=kOutput, calls=%fused_computation.72 | convolution fusion | flops 5435817984 | bytes 7077888 | tf_op jit(solution)/shard_map/dot_general | solution.py:233
  39.4 0.1 dynamic_slice.25
  39.6 0.1 dynamic_slice.22
  39.7 1.0 dynamic_slice.21
  40.7 0.9 dynamic-slice_bitcast_fusion
  41.6 0.8 dynamic-slice_bitcast_fusion.1
  42.5 0.1 pad_maximum_fusion.full_ref
  42.6 1.7 copy_bitcast_fusion.2
  44.3 1.4 maximum_bitcast_fusion.1
  45.7 0.0 copy-start.9
  45.7 0.0 copy-start.4
  45.7 0.0 copy-start.7
  45.7 7.2 %all-to-all-done.slab_ref = f32[4,2,2,16,3840]{4,3,2,1,0:T(8,128)} async-done(((f32[4,2,2,16,3840]{4,3,2,1,0:T(8,128)}), f32[4,2,2,16,3840]{4,3,2,1,0:T(8,128)}, u32[]{:S(2)}, u32[]{:S(2)}) %all-to-all-start) | async-done | bytes 3932192 | tf_op jit(solution)/shard_map/all_to_all | solution.py:506
  52.9 5.9 %all-to-all-start.1 = ((f32[4,2,2,8,3840]{4,3,2,1,0:T(8,128)}), f32[4,2,2,8,3840]{4,3,2,1,0:T(8,128)S(1)}, u32[]{:S(2)}, u32[]{:S(2)}) async-start(f32[4,2,2,8,3840]{4,3,2,1,0:T(8,128)} %maximum_bitcast_fusion.1), calls=%async_computation.1 | async-start | bytes 3932160 | tf_op jit(solution)/shard_map/all_to_all | solution.py:506
  58.8 0.0 copy-done.9
  58.8 0.0 copy-done.4
  58.8 0.0 copy-done.7
  58.8 0.0 copy-start.5
  58.8 0.9 copy-done.5
  59.8 13.7 %shard_map.122.earlier_ref = f32[2,2,4,24,3840]{4,3,2,1,0:T(8,128)S(1)} custom-call(f32[4,2,2,16,3840]{4,3,2,1,0:T(8,128)} %all-to-all-done.slab_ref, f32[1,3840]{1,0:T(1,128)S(1)} %reshape.37.keep_ref, f32[2,45,128]{2,1,0:T(8,128)S(1)} %copy-done.7, bf16[2,256,256]{2,1,0:T(8,128)(2,1)S(1)} %copy-done.5, bf16[2,256,256]{2,1,0:T(8,128)(2,1)S(1)} %copy-done.4, ...), custom_call_target="tpu_custom_call" | custom-call | flops 4529848320 | bytes 4194304 | tf_op jit(solution)/shard_map/pallas_call | solution.py:193
  73.5 0.0 copy-start.1
  73.5 2.5 %copy-done.1 = f32[2,2,4,24,3840]{4,3,2,1,0:T(8,128)} copy-done((f32[2,2,4,24,3840]{4,3,2,1,0:T(8,128)}, f32[2,2,4,24,3840]{4,3,2,1,0:T(8,128)S(1)}, u32[]{:S(2)}) %copy-start.1) | copy-done | bytes 5898264
  76.0 5.4 %all-to-all-done.1.slab_ref = f32[4,2,2,8,3840]{4,3,2,1,0:T(8,128)S(1)} async-done(((f32[4,2,2,8,3840]{4,3,2,1,0:T(8,128)}), f32[4,2,2,8,3840]{4,3,2,1,0:T(8,128)S(1)}, u32[]{:S(2)}, u32[]{:S(2)}) %all-to-all-start.1) | async-done | bytes 1966112 | tf_op jit(solution)/shard_map/all_to_all | solution.py:506
  81.4 0.0 copy-start.2
  81.4 2.7 %copy-done.2 = f32[2,2,4,24,3840]{4,3,2,1,0:T(8,128)S(1)} copy-done((f32[2,2,4,24,3840]{4,3,2,1,0:T(8,128)S(1)}, f32[2,2,4,24,3840]{4,3,2,1,0:T(8,128)}, u32[]{:S(2)}) %copy-start.2) | copy-done | bytes 5898264
  84.1 0.0 copy-start.6
  84.1 0.9 copy-done.6
  85.0 6.0 %shard_map.123.rhs_ref = f32[2,2,4,24,3840]{4,3,2,1,0:T(8,128)S(1)} custom-call(f32[4,2,2,8,3840]{4,3,2,1,0:T(8,128)S(1)} %all-to-all-done.1.slab_ref, f32[1,3840]{1,0:T(1,128)S(1)} %reshape.37.keep_ref, f32[2,45,128]{2,1,0:T(8,128)S(1)} %copy-done.7, bf16[2,256,256]{2,1,0:T(8,128)(2,1)S(1)} %copy-done.6, ...), custom_call_target="tpu_custom_call", output_to_operand_aliasing={{}: (5, {})} | custom-call | flops 2264924160 | bytes 2097152 | tf_op jit(solution)/shard_map/pallas_call | solution.py:193
  91.1 0.0 copy-start.3
  91.1 2.5 %copy-done.3 = f32[2,2,4,24,3840]{4,3,2,1,0:T(8,128)} copy-done((f32[2,2,4,24,3840]{4,3,2,1,0:T(8,128)}, f32[2,2,4,24,3840]{4,3,2,1,0:T(8,128)S(1)}, u32[]{:S(2)}) %copy-start.3) | copy-done | bytes 5898264
  93.6 136.2 %shard_map.124 = f32[4,96,3840]{2,1,0:T(8,128)S(1)} custom-call(f32[2,2,4,24,3840]{4,3,2,1,0:T(8,128)} %copy-done.3, f32[256,192]{1,0:T(8,128)S(1)} %maximum_select_fusion.local_ref, f32[2,128,128]{2,1,0:T(8,128)S(1)} %maximum_select_fusion.2.step_ref, f32[192,448]{1,0:T(8,128)S(1)} %pad_maximum_fusion.full_ref), custom_call_target="tpu_custom_call" | custom-call | tf_op jit(solution)/shard_map/pallas_call | solution.py:456
  229.8 3.0 %slice_bitcast_fusion = (f32[2,1,96,3840]{3,2,1,0:T(8,128)}, f32[2,1,96,3840]{3,2,1,0:T(8,128)}) fusion(f32[4,96,3840]{2,1,0:T(8,128)S(1)} %shard_map.124), kind=kLoop, calls=%fused_computation.1 | loop fusion | bytes 11796480
  (7 shorter events, 0.1 us)
Async XLA Ops:
  0.6 27.2 %copy-start = (f32[6,128,128]{2,1,0:T(8,128)S(1)}, f32[6,128,128]{2,1,0:T(8,128)}, u32[]{:S(2)}) copy-start(f32[6,128,128]{2,1,0:T(8,128)} %param.14) | copy-start | bytes 1179652
  5.3 47.6 %all-to-all-start = ((f32[4,2,2,16,3840]{4,3,2,1,0:T(8,128)}), f32[4,2,2,16,3840]{4,3,2,1,0:T(8,128)}, u32[]{:S(2)}, u32[]{:S(2)}) async-start(f32[4,2,2,16,3840]{4,3,2,1,0:T(8,128)} %maximum_bitcast_fusion), calls=%async_computation | async-start | bytes 7864320 | tf_op jit(solution)/shard_map/all_to_all | solution.py:506
  10.1 2.1 copy-start.8
  45.7 13.1 %copy-start.9 = (s32[3840]{0:T(1024)S(1)}, s32[3840]{0:T(1024)}, u32[]{:S(2)}) copy-start(s32[3840]{0:T(1024)} %param.13) | copy-start | bytes 46084
  45.7 13.1 %copy-start.4 = (bf16[2,256,256]{2,1,0:T(8,128)(2,1)S(1)}, bf16[2,256,256]{2,1,0:T(8,128)(2,1)}, u32[]{:S(2)}) copy-start(bf16[2,256,256]{2,1,0:T(8,128)(2,1)} %constant.76.clone.wfwd_ref) | copy-start | bytes 786436
  45.7 13.1 %copy-start.7 = (f32[2,45,128]{2,1,0:T(8,128)S(1)}, f32[2,45,128]{2,1,0:T(8,128)}, u32[]{:S(2)}) copy-start(f32[2,45,128]{2,1,0:T(8,128)} %constant.74.clone.twist_ref) | copy-start | bytes 138244
  52.9 28.5 %all-to-all-start.1 = ((f32[4,2,2,8,3840]{4,3,2,1,0:T(8,128)}), f32[4,2,2,8,3840]{4,3,2,1,0:T(8,128)S(1)}, u32[]{:S(2)}, u32[]{:S(2)}) async-start(f32[4,2,2,8,3840]{4,3,2,1,0:T(8,128)} %maximum_bitcast_fusion.1), calls=%async_computation.1 | async-start | bytes 3932160 | tf_op jit(solution)/shard_map/all_to_all | solution.py:506
  58.8 1.0 copy-start.5
  73.5 2.5 %copy-start.1 = (f32[2,2,4,24,3840]{4,3,2,1,0:T(8,128)}, f32[2,2,4,24,3840]{4,3,2,1,0:T(8,128)S(1)}, u32[]{:S(2)}) copy-start(f32[2,2,4,24,3840]{4,3,2,1,0:T(8,128)S(1)} %shard_map.122.earlier_ref) | copy-start | bytes 17694724
  81.4 2.7 %copy-start.2 = (f32[2,2,4,24,3840]{4,3,2,1,0:T(8,128)S(1)}, f32[2,2,4,24,3840]{4,3,2,1,0:T(8,128)}, u32[]{:S(2)}) copy-start(f32[2,2,4,24,3840]{4,3,2,1,0:T(8,128)} %copy-done.1) | copy-start | bytes 17694724
  84.1 0.9 copy-start.6
  91.1 2.5 %copy-start.3 = (f32[2,2,4,24,3840]{4,3,2,1,0:T(8,128)}, f32[2,2,4,24,3840]{4,3,2,1,0:T(8,128)S(1)}, u32[]{:S(2)}) copy-start(f32[2,2,4,24,3840]{4,3,2,1,0:T(8,128)S(1)} %shard_map.123.rhs_ref) | copy-start | bytes 17694724
